TPU v7x, 512 devices: a whole 4x8x8 slice. The times are simulated.
512 devices in a mesh: wave: 128 (over z, y, core), lev: 4 (over x).
Axes of the slice: x: 4, y: 8, z: 8, core: 2. Of those that a mesh axis runs over, the one named last changes fastest.
Arguments:
- fine_state: float32 [8, 3, 2, 384, 769], P('lev', None, None, 'wave'), may hold values from -6 to 6
- fold_pairs: int32 [384], replicated, may hold values from 0 to 383, each once
- legendre: bfloat16 [384, 1536, 769], P('wave', 'lev'), may hold values from -0.21875 to 0.21875
- gauss_weights: float32 [1536], P('lev'), may hold values from 0.5 to 3
- grid_coef: float32 [8, 2560], replicated, may hold values from -4 to 4
- modes_from: float32 [8, 8], replicated
- modes_to: float32 [8, 8], replicated, as said below
- mode_rates: float32 [8], replicated, may hold values from 0.2 to 20
Outputs:
- corrected: float32 [8, 2, 2, 384, 769], P('lev', None, None, 'wave')
- fine_tend: float32 [8, 3, 2, 384, 769], P('lev', None, None, 'wave')
Inputs may be any that keep to these rules, and one draw needn't show every extreme that they name: Slot p holds zonal wavenumbers fold_pairs[p] and 767 - fold_pairs[p]; every value occurs once. modes_to is the inverse of modes_from.
All inputs are finite; a program needn't handle non-finite values.
Results may differ from a plain program's by a relative error of at most 0.02.
Values may be sent and summed in bfloat16 or wider, within the bound.
A program may use at most 64 MiB of HBM per device.

v0:
```python
import math

import jax
import jax.numpy as jnp
from jax import lax
from jax.sharding import PartitionSpec as P

STEP_HALF = 0.5
quad_weights = ((5.0 / 24.0, 1.0 / 3.0, -1.0 / 24.0), (-1.0 / 24.0, 1.0 / 3.0, 5.0 / 24.0))
HIGHEST = lax.Precision.HIGHEST


def fourier_table(waves, points, amplitude):
    steps = jnp.arange(points, dtype=jnp.int32)
    turns = waves[:, :, None] * steps[None, None, :] % points
    angles = turns.astype(jnp.float32) * (2.0 * math.pi / points)
    return jnp.stack([jnp.cos(angles) * amplitude, -jnp.sin(angles) * amplitude]).astype(
        jnp.bfloat16
    )


def fine_rows(small_wave, fine_width):
    row_ids = jnp.arange(fine_width + 1, dtype=jnp.int32)[None, :]
    return row_ids < fine_width - small_wave[:, None]


def coarse_rows(small_wave, coarse):
    row_ids = jnp.arange(coarse, dtype=jnp.int32)[None, :]
    coarse_keep = row_ids < coarse - small_wave[:, None]
    degree = (small_wave[:, None] + row_ids).astype(jnp.float32)
    return (coarse_keep, degree)


def legendre_inverse(spectral, legendre_table, row_mask):
    split_spec = spectral[:, :, :, :, None, :] * row_mask[None, None, None]
    return jnp.einsum(
        "abcpmr,plr->abcpml", split_spec, legendre_table, preferred_element_type=jnp.float32
    ).astype(jnp.bfloat16)


def legendre_forward(returned, legendre_table, row_mask):
    members = jnp.einsum(
        "abcpml,plr->abcpmr", returned, legendre_table, preferred_element_type=jnp.float32
    )
    return jnp.sum(members * row_mask.astype(jnp.float32)[None, None, None], axis=4)


def grid_step(fourier, wave_table, coef, weights, factor):
    grid_field = jnp.einsum(
        "abcpmz,cpmk->abzk", fourier, wave_table, preferred_element_type=jnp.float32
    )
    product = (coef[:, None, None, :] * grid_field * grid_field).astype(jnp.bfloat16)
    returned = jnp.einsum(
        "abzk,cpmk->abcpmz", product, wave_table, preferred_element_type=jnp.float32
    )
    return (returned * (weights * factor)).astype(jnp.bfloat16)


def mix(matrix, values):
    return jnp.einsum("ql,lbcpr->qbcpr", matrix, values, precision=HIGHEST)


def per_device(
    fine_state, fold_pairs, legendre, gauss_weights, grid_coef, modes_from, modes_to, mode_rates
):
    n_wave = lax.axis_size("wave")
    wave_idx = lax.axis_index("wave")
    lev_idx = lax.axis_index("lev")
    lev_dev = fine_state.shape[0]
    pairs_dev = fine_state.shape[3]
    fine_width = fine_state.shape[4] - 1
    coarse = fine_width // 2
    longitudes = grid_coef.shape[1]
    band_size = legendre.shape[1] // n_wave
    small_wave = lax.dynamic_slice_in_dim(fold_pairs, wave_idx * pairs_dev, pairs_dev)
    first_member = fine_rows(small_wave, fine_width)
    member_mask = jnp.stack([first_member, jnp.logical_not(first_member)], 1).astype(jnp.bfloat16)
    coarse_keep, degree = coarse_rows(small_wave, coarse)
    keep_mask = coarse_keep[:, None, :].astype(jnp.bfloat16)
    keep_float = coarse_keep.astype(jnp.float32)
    fine_table = fourier_table(
        jnp.stack([fold_pairs, fine_width - 1 - fold_pairs], 1), longitudes, fine_width ** (-0.5)
    )
    coarse_table = fourier_table(fold_pairs[:, None], longitudes // 2, coarse ** (-0.5))
    coarse_leg = legendre[:, :, :coarse]
    coarse_coef = grid_coef[:, ::2]
    band_gauss = lax.dynamic_slice_in_dim(gauss_weights, wave_idx * band_size, band_size)
    local_to = lax.dynamic_slice_in_dim(modes_to, lev_idx * lev_dev, lev_dev, 1)
    local_from = lax.dynamic_slice_in_dim(modes_from, lev_idx * lev_dev, lev_dev, 1)
    mode_decay = lax.dynamic_slice_in_dim(mode_rates, lev_idx * lev_dev, lev_dev)

    def project(partial_sum):
        return mix(modes_to, partial_sum)

    def coarse_start(modes):
        gathered = lax.all_gather(modes, "lev", axis=0, tiled=True)
        levels = (mix(modes_from, gathered) * keep_float).astype(jnp.bfloat16)
        return legendre_inverse(levels, coarse_leg, keep_mask)

    def coarse_grid_step(fourier):
        return grid_step(
            fourier, coarse_table, coarse_coef, band_gauss, 2.0 * coarse / (longitudes // 2)
        )

    def coarse_finish(returned):
        partial_sum = legendre_forward(returned, coarse_leg, keep_mask)
        return lax.psum_scatter(
            project(partial_sum).astype(jnp.bfloat16), "lev", scatter_dimension=0, tiled=True
        ).astype(jnp.float32)

    def coarse_eval(modes):
        fourier = lax.all_to_all(
            coarse_start(modes), "wave", split_axis=5, concat_axis=3, tiled=True
        )
        returned = lax.all_to_all(
            coarse_grid_step(fourier), "wave", split_axis=3, concat_axis=5, tiled=True
        )
        return coarse_finish(returned)

    restricted = fine_state[..., :coarse] * keep_float
    fine_spec = lax.all_gather(fine_state.astype(jnp.bfloat16), "lev", axis=0, tiled=True)
    fine_fourier = legendre_inverse(fine_spec, legendre, member_mask)
    fine_fourier = lax.all_to_all(fine_fourier, "wave", split_axis=5, concat_axis=3, tiled=True)
    fine_back = lax.all_to_all(
        grid_step(fine_fourier, fine_table, grid_coef, band_gauss, 2.0 * fine_width / longitudes),
        "wave",
        split_axis=3,
        concat_axis=5,
        tiled=True,
    )
    fine_tend = lax.psum_scatter(
        legendre_forward(fine_back, legendre, member_mask).astype(jnp.bfloat16),
        "lev",
        scatter_dimension=0,
        tiled=True,
    ).astype(jnp.float32)
    restricted_tend = fine_tend[..., :coarse] * keep_float
    stacked = jnp.concatenate([restricted, restricted_tend], 1)
    both_modes = lax.psum_scatter(
        mix(local_to, stacked).astype(jnp.bfloat16), "lev", scatter_dimension=0, tiled=True
    ).astype(jnp.float32)
    nodes = fine_state.shape[1]
    old_state = both_modes[:, :nodes]
    old_tend = both_modes[:, nodes:]
    old_coarse = coarse_eval(old_state[:, 1:2])
    stiffness = (
        mode_decay[:, None, None, None]
        * (degree * (degree + 1.0) / (coarse * (coarse + 1.0)))[None, None]
    )
    source = old_tend - stiffness[:, None] * old_state
    integral_mid = (
        quad_weights[0][0] * source[:, 0]
        + quad_weights[0][1] * source[:, 1]
        + quad_weights[0][2] * source[:, 2]
    )
    integral_end = (
        quad_weights[1][0] * source[:, 0]
        + quad_weights[1][1] * source[:, 1]
        + quad_weights[1][2] * source[:, 2]
    )
    divisor = 1.0 + STEP_HALF * stiffness
    next_mid = (old_state[:, 0] + STEP_HALF * stiffness * old_state[:, 1] + integral_mid) / divisor
    coarse_fresh = coarse_eval(next_mid[:, None])
    next_end = (
        next_mid
        + STEP_HALF * (coarse_fresh[:, 0] - old_coarse[:, 0])
        + STEP_HALF * stiffness * old_state[:, 2]
        + integral_end
    ) / divisor
    change = jnp.stack([next_mid - old_state[:, 1], next_end - old_state[:, 2]], 1)
    lifted = lax.psum_scatter(
        mix(local_from, change).astype(jnp.bfloat16), "lev", scatter_dimension=0, tiled=True
    ).astype(jnp.float32)
    corrected = fine_state[:, 1:] + jnp.pad(
        lifted, ((0, 0), (0, 0), (0, 0), (0, 0), (0, fine_width + 1 - coarse))
    )
    return (corrected, fine_tend)


def solution(mesh):
    placed = (
        P("lev", None, None, "wave", None),
        P(),
        P("wave", "lev", None),
        P("lev"),
        P(),
        P(),
        P(),
        P(),
    )
    return jax.shard_map(
        per_device,
        mesh=mesh,
        in_specs=placed,
        out_specs=(P("lev", None, None, "wave", None), P("lev", None, None, "wave", None)),
        check_vma=False,
    )
```

profile of v0, /device:TPU:1, one launch (start us, length us, event | category | flops | bytes accessed | tf_op | source)
XLA Modules:
  0.0 516.8 jit_solution(16940937382540160421)
XLA Ops:
  7.2 1.3 broadcast_subtract_fusion.2
  9.1 0.9 convert_element_type.212
  10.0 10.5 %all_gather.9 = bf16[8,3,2,3,769]{4,2,3,1,0:T(2,128)(2,1)S(1)} all-gather(bf16[2,3,2,3,769]{4,2,3,1,0:T(2,128)(2,1)S(1)} %convert_element_type.212), channel_id=1, replica_groups=mesh['wave'=128,'lev'=4] {'lev'}, dimensions={0}, use_global_device_ids=true | all-gather | bytes 276840 | tf_op jit(solution)/shard_map/all_gather | solution.py:121
  21.2 2.7 fusion.53
  23.9 9.3 %copy.98 = bf16[8,3,2,3,2,384]{0,4,2,1,3,5:T(2,128)(2,1)S(1)} copy(bf16[8,3,2,3,2,384]{5,0,4,2,1,3:T(8,128)(2,1)} %fusion.53) | data formatting | bytes 442368 | tf_op jit(solution)/shard_map/convert_element_type | solution.py:38
  33.2 3.7 reshape.468
  36.9 21.6 %all-to-all-start = ((bf16[128,2,432]{2,1,0:T(2,128)(2,1)}), bf16[128,2,432]{2,1,0:T(2,128)(2,1)}, u32[]{:S(2)}, u32[]{:S(2)}) async-start(bf16[128,2,432]{2,1,0:T(2,128)(2,1)} %reshape.468), calls=%async_computation | async-start | bytes 524288 | tf_op jit(solution)/shard_map/all_to_all | solution.py:123
  58.6 35.6 %multiply_convert_fusion.1 = (bf16[1,384,2,2560]{3,1,2,0:T(8,128)(2,1)}, bf16[1,384,2,2560]{3,1,2,0:T(8,128)(2,1)}) fusion(s32[384,2]{0,1:T(2,128)S(1)} %pad_add_fusion), kind=kLoop, calls=%fused_computation.9 | loop fusion | flops 27525120 | bytes 7867392 | tf_op jit(solution)/shard_map/convert.4
  94.2 2.0 slice.58
  96.2 1.3 dynamic-slice
  98.8 1.3 dynamic-slice_multiply_fusion
  100.8 7.0 %reshape.469 = bf16[384,3,3,2,2,8]{5,4,3,2,1,0:T(2,128)(2,1)S(1)} reshape(bf16[128,2,432]{2,1,0:T(2,128)(2,1)} %all-to-all-done) | data formatting | bytes 442368
  107.8 2.4 copy.100
  110.3 4.1 fusion.103
  114.3 3.3 fusion.50
  117.7 8.4 %copy.102 = bf16[8,3,2,384,2,3]{0,4,5,2,1,3:T(2,128)(2,1)S(1)} copy(bf16[8,3,2,384,2,3]{3,0,5,1,4,2:T(8,128)(2,1)} %fusion.50) | data formatting | bytes 442368 | tf_op jit(solution)/shard_map/convert_element_type | solution.py:56
  126.1 3.7 reshape.470
  129.8 13.9 %all-to-all-start.1 = ((bf16[128,2,432]{2,1,0:T(2,128)(2,1)}), bf16[128,2,432]{2,1,0:T(2,128)(2,1)S(1)}, u32[]{:S(2)}, u32[]{:S(2)}) async-start(bf16[128,2,432]{2,1,0:T(2,128)(2,1)} %reshape.470), calls=%async_computation.1 | async-start | bytes 524288 | tf_op jit(solution)/shard_map/all_to_all | solution.py:124
  143.7 11.3 %multiply_convert_fusion.3 = (bf16[1,384,1280]{2,1,0:T(8,128)(2,1)}, bf16[1,384,1280]{2,1,0:T(8,128)(2,1)}) fusion(s32[384]{0:T(512)} %param.9), kind=kLoop, calls=%fused_computation.31 | loop fusion | flops 6881280 | bytes 1967616 | tf_op jit(solution)/shard_map/convert.2
  155.0 3.9 all-to-all-done.1
  158.9 4.8 reshape.471
  163.7 5.6 %copy.104 = bf16[8,3,2,3,2,128,3]{0,4,6,5,3,2,1:T(2,128)(2,1)S(1)} copy(bf16[8,3,2,3,2,128,3]{0,4,6,2,1,3,5:T(2,128)(2,1)} %bitcast.281) | data formatting | bytes 442368 | tf_op jit(solution)/shard_map/all_to_all | solution.py:124
  169.3 3.8 fusion.36
  174.0 46.5 %all-reduce.12.cloned.1.call-done = bf16[8,3,2,3,769]{4,0,3,2,1:T(8,128)(2,1)} async-done(((bf16[8,3,2,3,769]{4,0,3,2,1:T(8,128)(2,1)}), bf16[8,3,2,3,769]{4,0,3,2,1:T(8,128)(2,1)}) %all-reduce.12.cloned.1.call-update) | async-done | bytes 221488
  220.6 1.0 dynamic-slice_convert_fusion
  221.7 1.3 convolution_convert_fusion
  223.0 52.8 %all-reduce.14.cloned.1.call-done = bf16[8,6,2,3,384]{4,0,3,2,1:T(8,128)(2,1)} async-done(((bf16[8,6,2,3,384]{4,0,3,2,1:T(8,128)(2,1)}), bf16[8,6,2,3,384]{4,0,3,2,1:T(8,128)(2,1)}) %all-reduce.14.cloned.1.call-update) | async-done | bytes 221200
  275.9 1.0 dynamic-slice_convert_fusion.1
  277.0 9.0 %all_gather.10 = f32[8,1,2,3,384]{4,2,3,1,0:T(2,128)S(1)} all-gather(f32[2,1,2,3,384]{4,2,3,1,0:T(2,128)S(1)} %copy.107), channel_id=1, replica_groups=mesh['wave'=128,'lev'=4] {'lev'}, dimensions={0}, use_global_device_ids=true | all-gather | bytes 92160 | tf_op jit(solution)/shard_map/all_gather | solution.py:96
  286.4 1.7 copy.110
  288.1 19.3 %all-to-all-start.2 = ((bf16[8,1,2,3,1,384]{0,2,3,4,1,5:T(2,128)(2,1)}), bf16[8,1,2,3,1,384]{0,2,3,4,1,5:T(2,128)(2,1)S(1)}, u32[]{:S(2)}, u32[]{:S(2)}) async-start(bf16[8,1,2,3,1,384]{0,2,3,4,1,5:T(2,128)(2,1)} %copy.110), calls=%async_computation.2 | async-start | bytes 1179648 | tf_op jit(solution)/shard_map/all_to_all | solution.py:112
  307.5 9.9 %all_gather.11 = f32[8,1,2,3,384]{4,2,3,1,0:T(2,128)S(1)} all-gather(f32[2,1,2,3,384]{4,2,3,1,0:T(2,128)S(1)} %copy.118), channel_id=1, replica_groups=mesh['wave'=128,'lev'=4] {'lev'}, dimensions={0}, use_global_device_ids=true | all-gather | bytes 92160 | tf_op jit(solution)/shard_map/all_gather | solution.py:96
  317.8 1.7 copy.120
  319.5 9.9 %all-to-all-done.2 = bf16[8,1,2,3,1,384]{0,2,3,4,1,5:T(2,128)(2,1)S(1)} async-done(((bf16[8,1,2,3,1,384]{0,2,3,4,1,5:T(2,128)(2,1)}), bf16[8,1,2,3,1,384]{0,2,3,4,1,5:T(2,128)(2,1)S(1)}, u32[]{:S(2)}, u32[]{:S(2)}) %all-to-all-start.2) | async-done | bytes 36896 | tf_op jit(solution)/shard_map/all_to_all | solution.py:112
  329.4 5.8 %all-to-all-start.4 = ((bf16[8,1,2,3,1,384]{0,2,3,4,1,5:T(2,128)(2,1)}), bf16[8,1,2,3,1,384]{0,2,3,4,1,5:T(2,128)(2,1)S(1)}, u32[]{:S(2)}, u32[]{:S(2)}) async-start(bf16[8,1,2,3,1,384]{0,2,3,4,1,5:T(2,128)(2,1)} %copy.120), calls=%async_computation.4 | async-start | bytes 1179648 | tf_op jit(solution)/shard_map/all_to_all | solution.py:112
  336.1 3.2 fusion.91
  339.3 1.7 copy.114
  341.0 16.2 %all-to-all-done.4 = bf16[8,1,2,3,1,384]{0,2,3,4,1,5:T(2,128)(2,1)S(1)} async-done(((bf16[8,1,2,3,1,384]{0,2,3,4,1,5:T(2,128)(2,1)}), bf16[8,1,2,3,1,384]{0,2,3,4,1,5:T(2,128)(2,1)S(1)}, u32[]{:S(2)}, u32[]{:S(2)}) %all-to-all-start.4) | async-done | bytes 36896 | tf_op jit(solution)/shard_map/all_to_all | solution.py:112
  357.2 5.4 %all-to-all-start.3 = ((bf16[8,1,2,384,1,3]{0,2,5,4,1,3:T(2,128)(2,1)}), bf16[8,1,2,384,1,3]{0,2,5,4,1,3:T(2,128)(2,1)S(1)}, u32[]{:S(2)}, u32[]{:S(2)}) async-start(bf16[8,1,2,384,1,3]{0,2,5,4,1,3:T(2,128)(2,1)} %copy.114), calls=%async_computation.3 | async-start | bytes 1179648 | tf_op jit(solution)/shard_map/all_to_all | solution.py:115
  363.5 3.2 fusion.88
  366.7 1.7 copy.124
  368.4 16.2 %all-to-all-done.3 = bf16[8,1,2,384,1,3]{0,2,5,4,1,3:T(2,128)(2,1)S(1)} async-done(((bf16[8,1,2,384,1,3]{0,2,5,4,1,3:T(2,128)(2,1)}), bf16[8,1,2,384,1,3]{0,2,5,4,1,3:T(2,128)(2,1)S(1)}, u32[]{:S(2)}, u32[]{:S(2)}) %all-to-all-start.3) | async-done | bytes 36896 | tf_op jit(solution)/shard_map/all_to_all | solution.py:115
  384.6 5.4 %all-to-all-start.5 = ((bf16[8,1,2,384,1,3]{0,2,5,4,1,3:T(2,128)(2,1)}), bf16[8,1,2,384,1,3]{0,2,5,4,1,3:T(2,128)(2,1)S(1)}, u32[]{:S(2)}, u32[]{:S(2)}) async-start(bf16[8,1,2,384,1,3]{0,2,5,4,1,3:T(2,128)(2,1)} %copy.124), calls=%async_computation.5 | async-start | bytes 1179648 | tf_op jit(solution)/shard_map/all_to_all | solution.py:115
  391.9 20.2 %all-to-all-done.5 = bf16[8,1,2,384,1,3]{0,2,5,4,1,3:T(2,128)(2,1)S(1)} async-done(((bf16[8,1,2,384,1,3]{0,2,5,4,1,3:T(2,128)(2,1)}), bf16[8,1,2,384,1,3]{0,2,5,4,1,3:T(2,128)(2,1)S(1)}, u32[]{:S(2)}, u32[]{:S(2)}) %all-to-all-start.5) | async-done | bytes 36896 | tf_op jit(solution)/shard_map/all_to_all | solution.py:115
  413.8 40.0 %all-reduce.18.cloned.1.call-done = (bf16[8,1,2,3,384]{4,0,3,2,1:T(8,128)(2,1)}, bf16[8,1,2,3,384]{4,0,3,2,1:T(8,128)(2,1)}) async-done(((bf16[8,1,2,3,384]{4,0,3,2,1:T(8,128)(2,1)}, bf16[8,1,2,3,384]{4,0,3,2,1:T(8,128)(2,1)}), (bf16[8,1,2,3,384]{4,0,3,2,1:T(8,128)(2,1)}, bf16[8,1,2,3,384]{4,0,3,2,1:T(8,128)(2,1)})) %all-reduce.18.cloned.1.call-update) | async-done | bytes 73744
  454.7 1.0 convolution_convert_fusion.1
  456.4 51.9 %all-reduce.16.cloned.1.call-done = bf16[8,2,2,3,384]{4,0,3,2,1:T(8,128)(2,1)} async-done(((bf16[8,2,2,3,384]{4,0,3,2,1:T(8,128)(2,1)}), bf16[8,2,2,3,384]{4,0,3,2,1:T(8,128)(2,1)}) %all-reduce.16.cloned.1.call-update) | async-done | bytes 73744
  508.4 0.9 constant_dynamic-slice_fusion
  (85 shorter events, 12.1 us)
Async XLA Ops:
  7.2 214.5 %copy-start = (f32[8,8]{1,0:T(8,128)S(1)}, f32[8,8]{1,0:T(8,128)}, u32[]{:S(2)}) copy-start(f32[8,8]{1,0:T(8,128)} %param.14) | copy-start | bytes 772
  8.5 0.5 copy-start.12
  23.9 34.6 %copy-start.6 = (s32[384]{0:T(512)S(1)}, s32[384]{0:T(512)}, u32[]{:S(2)}) copy-start(s32[384]{0:T(512)} %param.9) | copy-start | bytes 4612
  36.9 63.9 %all-to-all-start = ((bf16[128,2,432]{2,1,0:T(2,128)(2,1)}), bf16[128,2,432]{2,1,0:T(2,128)(2,1)}, u32[]{:S(2)}, u32[]{:S(2)}) async-start(bf16[128,2,432]{2,1,0:T(2,128)(2,1)} %reshape.468), calls=%async_computation | async-start | bytes 524288 | tf_op jit(solution)/shard_map/all_to_all | solution.py:123
  58.6 35.6 %copy-start.7 = (f32[8,2560]{1,0:T(8,128)S(1)}, f32[8,2560]{1,0:T(8,128)}, u32[]{:S(2)}) copy-start(f32[8,2560]{1,0:T(8,128)} %param.12) | copy-start | bytes 245764
  58.6 39.7 %copy-start.15 = (f32[8]{0:T(128)S(1)}, f32[8]{0:T(128)}, u32[]{:S(2)}) copy-start(f32[8]{0:T(128)} %param.15) | copy-start | bytes 100
  58.6 41.5 %copy-start.11 = (s32[3]{0:T(128)S(1)}, s32[3]{0:T(128)}, u32[]{:S(2)}) copy-start(s32[3]{0:T(128)} %get-tuple-element.14) | copy-start | bytes 40
  107.8 2.5 copy-start.2
  107.8 2.5 copy-start.8
  110.2 4.1 copy-start.3
  110.2 4.1 copy-start.16
  129.8 29.2 %all-to-all-start.1 = ((bf16[128,2,432]{2,1,0:T(2,128)(2,1)}), bf16[128,2,432]{2,1,0:T(2,128)(2,1)S(1)}, u32[]{:S(2)}, u32[]{:S(2)}) async-start(bf16[128,2,432]{2,1,0:T(2,128)(2,1)} %reshape.470), calls=%async_computation.1 | async-start | bytes 524288 | tf_op jit(solution)/shard_map/all_to_all | solution.py:124
  143.7 76.9 %all-reduce.12.cloned.1.call-start = ((), (), s32[]{:S(2)}) async-start(), calls=%async_computation.6 | async-start | bytes 516096
  163.7 5.6 %copy-start.1 = (bf16[3,384,769]{1,2,0:T(8,128)(2,1)S(1)}, bf16[3,384,769]{1,2,0:T(8,128)(2,1)}, u32[]{:S(2)}) copy-start(bf16[3,384,769]{1,2,0:T(8,128)(2,1)} %param.10) | copy-start | bytes 5315332
  163.7 5.6 %copy-start.4 = (f32[3,2,769]{2,1,0:T(2,128)S(1)}, f32[3,2,769]{2,1,0:T(2,128)}, u32[]{:S(2)}) copy-start(f32[3,2,769]{2,1,0:T(2,128)} %get-tuple-element.16) | copy-start | bytes 55372
  169.3 4.7 copy-start.13
  169.3 52.3 %slice-start = ((f32[2,3,2,3,769]{4,2,3,1,0:T(2,128)}), f32[2,3,2,3,384]{4,2,3,1,0:T(2,128)S(1)}, s32[]{:S(2)}) async-start(f32[2,3,2,3,769]{4,2,3,1,0:T(2,128)} %param.8), calls=%async_computation.10 | async-start | bytes 110592 | tf_op jit(solution)/shard_map/slice | solution.py:120
  169.3 53.6 %copy-start.14 = (f32[2]{0:T(128)S(1)}, f32[2]{0:T(128)}, u32[]{:S(2)}) copy-start(f32[2]{0:T(128)} %dynamic_slice.19) | copy-start | bytes 28
  169.3 116.7 %copy-start.9 = (f32[8,8]{1,0:T(8,128)S(1)}, f32[8,8]{1,0:T(8,128)}, u32[]{:S(2)}) copy-start(f32[8,8]{1,0:T(8,128)} %param.13) | copy-start | bytes 772
  173.9 102.0 %all-reduce.14.cloned.1.call-start = ((), (), s32[]{:S(2)}) async-start(), calls=%async_computation.7 | async-start | bytes 442368
  286.4 49.7 %copy-start.5 = (f32[8,1280]{1,0:T(8,128)S(1)}, f32[8,1280]{1,0:T(8,128)}, u32[]{:S(2)}) copy-start(f32[8,1280]{1,0:T(8,128)} %slice.58) | copy-start | bytes 122884
  286.4 49.7 %copy-start.17 = (f32[3]{0:T(128)S(1)}, f32[3]{0:T(128)}, u32[]{:S(2)}) copy-start(f32[3]{0:T(128)} %dynamic-slice_multiply_fusion) | copy-start | bytes 40
  288.1 41.3 %all-to-all-start.2 = ((bf16[8,1,2,3,1,384]{0,2,3,4,1,5:T(2,128)(2,1)}), bf16[8,1,2,3,1,384]{0,2,3,4,1,5:T(2,128)(2,1)S(1)}, u32[]{:S(2)}, u32[]{:S(2)}) async-start(bf16[8,1,2,3,1,384]{0,2,3,4,1,5:T(2,128)(2,1)} %copy.110), calls=%async_computation.2 | async-start | bytes 1179648 | tf_op jit(solution)/shard_map/all_to_all | solution.py:112
  329.4 27.8 %all-to-all-start.4 = ((bf16[8,1,2,3,1,384]{0,2,3,4,1,5:T(2,128)(2,1)}), bf16[8,1,2,3,1,384]{0,2,3,4,1,5:T(2,128)(2,1)S(1)}, u32[]{:S(2)}, u32[]{:S(2)}) async-start(bf16[8,1,2,3,1,384]{0,2,3,4,1,5:T(2,128)(2,1)} %copy.120), calls=%async_computation.4 | async-start | bytes 1179648 | tf_op jit(solution)/shard_map/all_to_all | solution.py:112
  357.2 27.4 %all-to-all-start.3 = ((bf16[8,1,2,384,1,3]{0,2,5,4,1,3:T(2,128)(2,1)}), bf16[8,1,2,384,1,3]{0,2,5,4,1,3:T(2,128)(2,1)S(1)}, u32[]{:S(2)}, u32[]{:S(2)}) async-start(bf16[8,1,2,384,1,3]{0,2,5,4,1,3:T(2,128)(2,1)} %copy.114), calls=%async_computation.3 | async-start | bytes 1179648 | tf_op jit(solution)/shard_map/all_to_all | solution.py:115
  363.5 27.1 %copy-start.10 = (f32[3,384]{1,0:T(4,128)S(1)}, f32[3,384]{1,0:T(4,128)}, u32[]{:S(2)}) copy-start(f32[3,384]{1,0:T(4,128)} %get-tuple-element.28) | copy-start | bytes 13828
  384.6 27.4 %all-to-all-start.5 = ((bf16[8,1,2,384,1,3]{0,2,5,4,1,3:T(2,128)(2,1)}), bf16[8,1,2,384,1,3]{0,2,5,4,1,3:T(2,128)(2,1)S(1)}, u32[]{:S(2)}, u32[]{:S(2)}) async-start(bf16[8,1,2,384,1,3]{0,2,5,4,1,3:T(2,128)(2,1)} %copy.124), calls=%async_computation.5 | async-start | bytes 1179648 | tf_op jit(solution)/shard_map/all_to_all | solution.py:115
  390.1 119.2 %slice-start.1 = ((f32[2,3,2,3,769]{4,2,3,1,0:T(2,128)}), f32[2,2,2,3,769]{4,2,3,1,0:T(2,128)S(1)}, s32[]{:S(2)}) async-start(f32[2,3,2,3,769]{4,2,3,1,0:T(2,128)} %param.8), calls=%async_computation.11 | async-start | bytes 172032 | tf_op jit(solution)/shard_map/slice | solution.py:174
  390.1 63.8 %all-reduce.18.cloned.1.call-start = ((), (), s32[]{:S(2)}) async-start(), calls=%async_computation.9 | async-start | bytes 147456
  413.8 94.6 %all-reduce.16.cloned.1.call-start = ((), (), s32[]{:S(2)}) async-start(), calls=%async_computation.8 | async-start | bytes 147456
Sparse Core Ops, SparseCore 0:
  174.0 46.5 all-reduce.11
  223.1 52.7 all-reduce.13
  413.9 39.9 all-reduce.17
  456.7 51.5 all-reduce.15
where the time goes:
time: 524 us; the launch traced here: 517 us
  waiting for transfers between devices  258 us (49%)
  starting transfers between devices  71.6 us (14%)
  local copies, waits for them, and re-layouts  61.6 us (12%)
  other arithmetic  55 us (10%)
  blocking collectives  29.4 us (6%)
  matrix products  25.9 us (5%)
  between operations  15.2 us (3%)
    unnamed x8, waiting for transfers between devices  191 us
    another operation x2, other arithmetic  46.9 us
    all_to_all x2, waiting for transfers between devices, coarse_eval(): lax.all_to_all(coarse_grid_step(fourier), 'wave', split_axis=3, concat_ax...  36.4 us
    all_to_all x2, waiting for transfers between devices, coarse_eval(): lax.all_to_all(coarse_start(modes), 'wave', split_axis=5, concat_axis=3,...  26.1 us
    all_to_all x2, starting transfers between devices, coarse_eval(): lax.all_to_all(coarse_start(modes), 'wave', split_axis=5, concat_axis=3,...  25.1 us
    unnamed x44, local copies, waits for them, and re-layouts  23.2 us
    all_to_all x1, starting transfers between devices, per_device(): lax.all_to_all(fine_fourier, 'wave', split_axis=5, concat_axis=3, tiled=T...  21.6 us
    all_gather x2, blocking collectives, coarse_start(): gathered = lax.all_gather(modes, 'lev', axis=0, tiled=True)  18.9 us
  transfers between devices with their start and end apart: 10, of which 9 were waited for; matrix products, arithmetic and copies ran while one was open for 13% of the time, Pallas kernels for 0%

commit v1 on v0

v1 whole, which is shorter than its diff:
```python
import functools
import math

import jax
import jax.numpy as jnp
import ml_dtypes
import numpy as np
from jax import lax
from jax.experimental import pallas as pl
from jax.experimental.pallas import tpu as pltpu
from jax.sharding import PartitionSpec as P

F32 = jnp.float32
BF16 = jnp.bfloat16
HIGHEST = lax.Precision.HIGHEST
MESH = pl.DeviceIdType.MESH

NLON, LEV, WAVES, ROWS, NC = 2560, 8, 768, 769, 384
HALF, CHALF = NLON // 2, NLON // 4
NZ, ND, NT = 8, 16, 4
FACTOR = 2.0 * WAVES / NLON
QUAD = ((5.0 / 24.0, 1.0 / 3.0, -1.0 / 24.0), (-1.0 / 24.0, 1.0 / 3.0, 5.0 / 24.0))


def table(waves, points, amplitude, count):
    turns = np.outer(waves, np.arange(count)) % points
    angles = turns * (2.0 * math.pi / points)
    return np.concatenate([np.cos(angles), -np.sin(angles)], 0).reshape(2, len(waves), count) * amplitude


def tables():
    t = np.arange(192)
    fine, coarse = [], []
    for parity in (0, 1):
        low = 2 * t + parity
        high = (WAVES - 2 - 2 * t) + parity
        fine.append(table(np.concatenate([low, high]), NLON, WAVES**-0.5, HALF).reshape(768, HALF))
        part = table(low, NLON // 2, NC**-0.5, CHALF)
        coarse.append(np.concatenate([part, np.zeros_like(part)], 1).reshape(768, CHALF))
    as_bf16 = lambda parts: np.stack(parts).astype(np.float32).astype(ml_dtypes.bfloat16)
    return as_bf16(fine), as_bf16(coarse)


def selectors():
    to_rows = np.zeros((96, 8), np.float32)
    to_mask = np.zeros((96, 64), np.float32)
    to_cols = np.zeros((8, 64), np.float32)
    for lev in range(4):
        for c in range(2):
            for rho in range(8):
                col = lev * 16 + c * 8 + rho
                to_cols[lev * 2 + rho % 2, col] = 1
                node = rho // 2
                for q in range(8):
                    if node < 3:
                        to_mask[node * 16 + c * 8 + q, col] = 1
                        to_mask[48 + c * 8 + q, col] = QUAD[0][node]
                        to_mask[64 + c * 8 + q, col] = QUAD[1][node]
                    else:
                        to_mask[80 + c * 8 + q, col] = 1
    for row in range(96):
        to_rows[row, row % 8] = 1
    mix_cols = np.zeros((8, 16), np.float32)
    mix_rows = np.zeros((208, 8), np.float32)
    mix_mask = np.zeros((208, 16), np.float32)
    for c in range(2):
        for q in range(8):
            mix_cols[q, c * 8 + q] = 1
            for a in range(8):
                mix_rows[c * 8 + a, a] = 1
                mix_mask[c * 8 + a, c * 8 + q] = 1
                for p in range(3):
                    row = 16 + p * 64 + (a // 2) * 16 + p * 4 + (a % 2) * 2 + c
                    mix_rows[row, a] = 1
                    mix_mask[row, c * 8 + q] = 1
    return to_rows, to_mask, to_cols, mix_rows, mix_mask, mix_cols


def dot(a, b, precision=None):
    return lax.dot_general(a, b, (((1,), (0,)), ((), ())), precision=precision, preferred_element_type=F32)


def dot_nt(a, b):
    return lax.dot_general(a, b, (((1,), (1,)), ((), ())), preferred_element_type=F32)


def kernel(
    fs, leg_hbm, fold_s, fold_col, gauss_s, rates_s, coef, mto, mfrom, tf_hbm, tc_hbm,
    to_rows, to_mask, to_cols, mix_rows, mix_mask, mix_cols,
    corr, tend_out,
    leg, tf, tc, xf, gat, m0s, m1s, onehot, perm, permt, coefx, ccoefx, wto, wmix,
    s1, r1, stage, s2, r2, s3, r3, s4, r4, vbuf, s5, r5, states, oldp, lift,
    s6, r6, cstage, s7, r7, s8, r8, s9, r9, s10, r10,
    load_sem, z_send, z_recv, d_send, d_recv, lev_send, lev_recv,
):
    w = lax.axis_index("wave")
    t = lax.axis_index("lev")
    z, d = w // ND, w % ND

    loads = [
        pltpu.make_async_copy(leg_hbm, leg, load_sem.at[0]),
        pltpu.make_async_copy(tf_hbm, tf, load_sem.at[1]),
        pltpu.make_async_copy(tc_hbm, tc, load_sem.at[2]),
    ]
    for load in loads:
        load.start()

    barrier = pltpu.get_barrier_semaphore()

    def lev_dev(k):
        return {"lev": lax.rem(t + k, NT)}

    def z_dev(k):
        return {"wave": lax.rem(z + k, NZ) * ND + d}

    def d_dev(k):
        return {"wave": z * ND + lax.rem(d + k, ND)}

    groups = ((NT, lev_dev), (NZ, z_dev), (ND, d_dev))
    for count, dev in groups:
        @pl.loop(1, count)
        def _(k):
            pl.semaphore_signal(barrier, inc=1, device_id=dev(k), device_id_type=MESH)

    def lev_copy(k, src, dst, row):
        return pltpu.make_async_remote_copy(
            src_ref=src, dst_ref=dst, send_sem=lev_send.at[row, k], recv_sem=lev_recv.at[row, k],
            device_id=lev_dev(k), device_id_type=MESH)

    def z_copy(k, src, dst, row):
        return pltpu.make_async_remote_copy(
            src_ref=src.at[lax.rem(z + k, NZ)], dst_ref=dst.at[z], send_sem=z_send.at[row, k],
            recv_sem=z_recv.at[row, k], device_id=z_dev(k), device_id_type=MESH)

    def d_copy(k, src, dst, row):
        return pltpu.make_async_remote_copy(
            src_ref=src.at[lax.rem(d + k, ND)], dst_ref=dst.at[d], send_sem=d_send.at[row, k],
            recv_sem=d_recv.at[row, k], device_id=d_dev(k), device_id_type=MESH)

    def gather_copy(k, buf, row):
        return lev_copy(k, buf.at[t], buf.at[t], row)

    def scatter_copy(k, src, dst, row):
        return lev_copy(k, src.at[lax.rem(t + k, NT)], dst.at[t], row)

    def start(count, make):
        @pl.loop(1, count)
        def _(k):
            make(k).start()

    def arrive(count, make):
        @pl.loop(1, count)
        def _(k):
            make(k).wait_recv()

    def sent(count, make):
        @pl.loop(1, count)
        def _(k):
            make(k).wait_send()

    for p in range(3):
        for c in range(2):
            for a in range(2):
                for b in range(3):
                    xf[p, pl.ds(c * 8 + b * 2 + a, 1), :] = fs[a, b, p, pl.ds(c, 1), :]
                xf[p, pl.ds(c * 8 + 6 + a, 1), :] = fs[a, 1, p, pl.ds(c, 1), :]
    gat[t] = xf[...].astype(BF16)
    pl.semaphore_wait(barrier, (NT - 1) + (NZ - 1) + (ND - 1))
    e1 = lambda k: gather_copy(k, gat, 0)
    start(NT, e1)

    folds = [fold_s[w * 3 + p] for p in range(3)]
    rho = lax.rem(lax.broadcasted_iota(jnp.int32, (16, ROWS), 0), 8)
    row_r = lax.broadcasted_iota(jnp.int32, (16, ROWS), 1)
    for p in range(3):
        first = jnp.where(row_r < WAVES - folds[p], 1.0, 0.0)
        keep = jnp.where(row_r < NC - folds[p], 1.0, 0.0)
        m0s[p] = jnp.where(rho < 6, first, keep)
        m1s[p] = jnp.where(rho < 6, 1.0 - first, 0.0)
    fold = fold_col[...]
    half_fold, odd = fold // 2, lax.rem(fold, 2)
    cols = lax.broadcasted_iota(jnp.int32, (NC, 2 * NC), 1)
    onehot[pl.ds(0, NC), :] = jnp.where(cols == half_fold + NC * odd, 1.0, 0.0).astype(BF16)
    onehot[pl.ds(NC, NC), :] = jnp.where(cols == 192 + half_fold + NC * (1 - odd), 1.0, 0.0).astype(BF16)
    pr = lax.broadcasted_iota(jnp.int32, (128, 128), 0)
    pc = lax.broadcasted_iota(jnp.int32, (128, 128), 1)
    perm[...] = jnp.where(pc == lax.rem(pr, NZ) * ND + pr // NZ, 1.0, 0.0).astype(BF16)
    permt[...] = jnp.where(pr == lax.rem(pc, NZ) * ND + pc // NZ, 1.0, 0.0).astype(BF16)
    for lev in range(NT):
        for n in range(4):
            coefx[pl.ds(lev * 8 + n * 2, 2), :] = coef[pl.ds(lev * 2, 2), :]
    sel_r = lax.broadcasted_iota(jnp.int32, (256, 128), 0)
    sel_c = lax.broadcasted_iota(jnp.int32, (256, 128), 1)
    even = jnp.where(sel_r == 2 * sel_c, 1.0, 0.0)
    chunks = jnp.concatenate([coef[:, pl.ds(n * 256, 256)] for n in range(10)], 0)
    picked = dot(chunks, even, HIGHEST)
    ccoef = jnp.concatenate([picked[n * 8 : n * 8 + 8] for n in range(10)], 1)
    for n in range(10):
        for lev in range(NT):
            for m in range(4):
                ccoefx[pl.ds(lev * 8 + m * 2, 2), pl.ds(n * 128, 128)] = picked[n * 8 + lev * 2 : n * 8 + lev * 2 + 2]
    wto[...] = dot(dot(to_rows[...], mto[...], HIGHEST), to_cols[...], HIGHEST) * to_mask[...]
    wmix[pl.ds(0, 208), :] = dot(dot(mix_rows[...], mfrom[...], HIGHEST), mix_cols[...], HIGHEST) * mix_mask[...]
    wmix[pl.ds(208, 16), :] = (
        dot(dot(mix_rows[pl.ds(0, 16), :], mto[...], HIGHEST), mix_cols[...], HIGHEST) * mix_mask[pl.ds(0, 16), :]
    )
    stage[...] = jnp.zeros_like(stage)
    cstage[...] = jnp.zeros_like(cstage)

    arrive(NT, e1)
    loads[0].wait()

    for p in range(3):
        x = gat[:, p].reshape(64, ROWS)
        k0 = jnp.concatenate([m0s[p].astype(BF16)] * 4, 0)
        k1 = jnp.concatenate([m1s[p].astype(BF16)] * 4, 0)
        f = dot(jnp.concatenate([x * k0, x * k1], 0), leg[p])
        s1[:, :, pl.ds(p * 128, 128)] = f.T.astype(BF16).reshape(NZ, 48, 128)
    e2a = lambda k: z_copy(k, s1, r1, 0)
    start(NZ, e2a)
    r1[z] = s1[z]

    for p in range(3):
        x = gat[:, p, :, pl.ds(0, NC)].reshape(64, NC).astype(F32)
        keep = m0s[p, pl.ds(6, 1), pl.ds(0, NC)]
        states[p] = dot(wto[pl.ds(0, 48), :], x, HIGHEST) * keep
    arrive(NZ, e2a)
    for j in range(3):
        o = dot(perm[...], r1[:, pl.ds(j * 16, 16), :].reshape(128, 384))
        for p in range(3):
            stage[:, pl.ds(j * 24 + p * 8, 8), :] = o[:, p * 128 : p * 128 + 128].reshape(ND, 8, 128)
    s2[...] = stage[...].astype(BF16)
    e2b = lambda k: d_copy(k, s2, r2, 0)
    start(ND, e2b)
    r2[d] = s2[d]
    loads[1].wait()
    loads[2].wait()
    arrive(ND, e2b)

    stage[...] = r2[...].astype(F32)
    turned = []
    for j in range(3):
        by_p = [stage[:, pl.ds(j * 24 + p * 8, 8), :].reshape(128, 128) for p in range(3)]
        turned.append(jnp.concatenate(by_p, 0).T)
    natural = []
    for c in range(2):
        rows = []
        for j in range(3):
            members = []
            for i in range(2):
                at = [i * 64 + lev * 16 + c * 8 for lev in range(NT)]
                members.append(jnp.concatenate([turned[j][r : r + 8] for r in at], 0))
            rows.append(jnp.concatenate(members, 1))
        x = jnp.concatenate(rows, 0).astype(BF16)
        natural.append(dot(x, onehot[...]).astype(BF16))
    weights = [gauss_s[z * 48 + j * 16 + d] * FACTOR for j in range(3)]

    def grid(x_even, x_odd, tab, width, coefs, reps):
        e = dot(x_even, tab[0])
        o = dot(x_odd, tab[1])
        low, high = e + o, e - o
        c_low = jnp.concatenate([coefs[:, pl.ds(0, width)]] * reps, 0)
        c_high = jnp.concatenate([coefs[:, pl.ds(width, width)]] * reps, 0)
        prod = jnp.concatenate([c_low * low * low, c_high * high * high], 0).astype(BF16)
        n = low.shape[0]
        back_e = dot_nt(prod, tab[0])
        back_o = dot_nt(prod, tab[1])
        return back_e[:n] + back_e[n:], back_o[:n] - back_o[n:]

    x_even = jnp.concatenate([n[:, :NC] for n in natural], 1)
    x_odd = jnp.concatenate([n[:, NC:] for n in natural], 1)
    fe, fo = grid(x_even, x_odd, tf, HALF, coefx, 3)
    ce, co = grid(x_even, x_odd, tc, CHALF, ccoefx, 3)
    row = lax.broadcasted_iota(jnp.int32, (96, 2 * NC), 0)
    is_coarse = lax.rem(row, 8) >= 6
    wt = jnp.where(row < 32, weights[0], jnp.where(row < 64, weights[1], weights[2]))
    be = (jnp.where(is_coarse, ce, fe) * wt).astype(BF16)
    bo = (jnp.where(is_coarse, co, fo) * wt).astype(BF16)
    slot = []
    for c in range(2):
        y = jnp.concatenate([be[:, c * NC : c * NC + NC], bo[:, c * NC : c * NC + NC]], 1)
        slot.append(dot_nt(y, onehot[...]))
    for j in range(3):
        pieces = []
        for i in range(2):
            for lev in range(NT):
                for c in range(2):
                    r = j * 32 + lev * 8
                    pieces.append(slot[c][r : r + 8, i * NC : i * NC + NC])
        back = jnp.concatenate(pieces, 0).T
        for p in range(3):
            stage[:, pl.ds(j * 24 + p * 8, 8), :] = back[p * 128 : p * 128 + 128].reshape(ND, 8, 128)
    s3[...] = stage[...].astype(BF16)
    e3a = lambda k: d_copy(k, s3, r3, 1)
    start(ND, e3a)
    r3[d] = s3[d]
    arrive(ND, e3a)
    stage[...] = r3[...].astype(F32)
    for j in range(3):
        by_p = [stage[:, pl.ds(j * 24 + p * 8, 8), :].reshape(128, 128) for p in range(3)]
        o = dot(permt[...], jnp.concatenate(by_p, 1).astype(BF16))
        s4[:, pl.ds(j * 16, 16), :] = o.astype(BF16).reshape(NZ, 16, 384)
    e3b = lambda k: z_copy(k, s4, r4, 1)
    start(NZ, e3b)
    r4[z] = s4[z]
    arrive(NZ, e3b)

    for p in range(3):
        x = r4[:, :, pl.ds(p * 128, 128)].reshape(NC, 128).astype(F32).T.astype(BF16)
        o = dot_nt(x, leg[p])
        k0 = jnp.concatenate([m0s[p]] * 4, 0)
        k1 = jnp.concatenate([m1s[p]] * 4, 0)
        part = o[:64] * k0 + o[64:] * k1
        s5[:, p] = part.astype(BF16).reshape(NT, 16, ROWS)
        keep = m0s[p, pl.ds(6, 1), pl.ds(0, NC)]
        mixed = dot(wto[pl.ds(48, 48), :], part[:, :NC] * keep, HIGHEST)
        vbuf[t, p] = mixed[:32].astype(BF16)
        oldp[p] = mixed[32:]
    e4 = lambda k: gather_copy(k, vbuf, 1)
    start(NT, e4)
    e4t = lambda k: scatter_copy(k, s5, r5, 2)
    start(NT, e4t)
    r5[t] = s5[t]
    arrive(NT, e4)

    mode = lax.rem(lax.broadcasted_iota(jnp.int32, (16, NC), 0), 8)
    rate = jnp.zeros((16, NC), F32)
    for q in range(8):
        rate = jnp.where(mode == q, rates_s[q], rate)
    col = lax.broadcasted_iota(jnp.int32, (16, NC), 1)
    lifted_mid = jnp.zeros((64, NC), F32)
    lifted_end = jnp.zeros((64, NC), F32)
    fourier, changes = [], []
    for p in range(3):
        degree = (col + folds[p]).astype(F32)
        stiff = rate * (degree * (degree + 1.0) / (NC * (NC + 1.0)))
        keep = m0s[p, pl.ds(6, 1), pl.ds(0, NC)]
        tend = (vbuf[0, p].astype(F32) + vbuf[1, p].astype(F32)) + (vbuf[2, p].astype(F32) + vbuf[3, p].astype(F32))
        old = [states[p, pl.ds(b * 16, 16), :] for b in range(3)]
        int_mid = tend[:16] - stiff * (QUAD[0][0] * old[0] + QUAD[0][1] * old[1] + QUAD[0][2] * old[2])
        int_end = tend[16:] - stiff * (QUAD[1][0] * old[0] + QUAD[1][1] * old[1] + QUAD[1][2] * old[2])
        inv = 1.0 / (1.0 + 0.5 * stiff)
        mid = (old[0] + 0.5 * stiff * old[1] + int_mid) * inv
        levels = (dot(wmix[pl.ds(0, 16), :], mid, HIGHEST) * keep).astype(BF16)
        fourier.append(dot(levels, leg[p, pl.ds(0, NC), :]))
        changes.append((mid - old[1], (mid + 0.5 * stiff * old[2] + int_end) * inv - old[2], 0.5 * inv))
    rest = jnp.zeros((80, NC), F32)
    s6[...] = jnp.concatenate(fourier + [rest], 0).T.astype(BF16).reshape(NZ, 48, 128)
    e5a = lambda k: z_copy(k, s6, r6, 2)
    start(NZ, e5a)
    r6[z] = s6[z]
    for p in range(3):
        place = wmix[pl.ds(16 + p * 64, 64), :]
        lifted_mid += dot(place, changes[p][0], HIGHEST)
        lifted_end += dot(place, changes[p][1], HIGHEST)
    lift[0] = lifted_mid.reshape(NT, 16, NC)
    lift[1] = lifted_end.reshape(NT, 16, NC)
    arrive(NZ, e5a)
    for j in range(3):
        o = dot(perm[...], r6[:, pl.ds(j * 16, 16), :].reshape(128, 128))
        cstage[:, pl.ds(j * 8, 8), :] = o.reshape(ND, 8, 128)
    s7[...] = cstage[...].astype(BF16)
    e5b = lambda k: d_copy(k, s7, r7, 2)
    start(ND, e5b)
    r7[d] = s7[d]
    arrive(NT, e4t)
    for p in range(3):
        total = (r5[0, p].astype(F32) + r5[1, p].astype(F32)) + (r5[2, p].astype(F32) + r5[3, p].astype(F32))
        for c in range(2):
            for a in range(2):
                for b in range(3):
                    r = c * 8 + b * 2 + a
                    tend_out[a, b, p, pl.ds(c, 1), :] = total[r : r + 1]
    arrive(ND, e5b)

    cstage[...] = r7[...].astype(F32)
    turned = [cstage[:, pl.ds(j * 8, 8), :].reshape(128, 128).T for j in range(3)]
    natural = []
    for c in range(2):
        rows = []
        for j in range(3):
            at = [p * 16 + c * 8 for p in range(3)]
            rows.append(jnp.concatenate([turned[j][r : r + 8] for r in at], 1))
        rows.append(jnp.zeros((8, NC), F32))
        x = jnp.concatenate(rows, 0).astype(BF16)
        natural.append(dot(x, onehot[pl.ds(0, NC), :]).astype(BF16))
    x_even = jnp.concatenate([n[:, :NC] for n in natural], 1)
    x_odd = jnp.concatenate([n[:, NC:] for n in natural], 1)
    e = dot(x_even, tc[0])
    o = dot(x_odd, tc[1])
    low, high = e + o, e - o
    c_low = jnp.concatenate([ccoef[:, :CHALF]] * 4, 0)
    c_high = jnp.concatenate([ccoef[:, CHALF:]] * 4, 0)
    prod = jnp.concatenate([c_low * low * low, c_high * high * high], 0).astype(BF16)
    back_e = dot_nt(prod, tc[0])
    back_o = dot_nt(prod, tc[1])
    row = lax.broadcasted_iota(jnp.int32, (32, 2 * NC), 0)
    wt = jnp.where(row < 8, weights[0], jnp.where(row < 16, weights[1], weights[2]))
    be = ((back_e[:32] + back_e[32:]) * wt).astype(BF16)
    bo = ((back_o[:32] - back_o[32:]) * wt).astype(BF16)
    slot = []
    for c in range(2):
        y = jnp.concatenate([be[:, c * NC : c * NC + NC], bo[:, c * NC : c * NC + NC]], 1)
        slot.append(dot_nt(y, onehot[pl.ds(0, NC), :]))
    for j in range(3):
        pieces = []
        for p in range(3):
            for c in range(2):
                pieces.append(slot[c][j * 8 : j * 8 + 8, p * 128 : p * 128 + 128])
        pieces.append(jnp.zeros((80, 128), F32))
        cstage[:, pl.ds(j * 8, 8), :] = jnp.concatenate(pieces, 0).T.reshape(ND, 8, 128)
    s8[...] = cstage[...].astype(BF16)
    e6a = lambda k: d_copy(k, s8, r8, 3)
    start(ND, e6a)
    r8[d] = s8[d]
    arrive(ND, e6a)
    cstage[...] = r8[...].astype(F32)
    for j in range(3):
        x = cstage[:, pl.ds(j * 8, 8), :].reshape(128, 128).astype(BF16)
        s9[:, pl.ds(j * 16, 16), :] = dot(permt[...], x).astype(BF16).reshape(NZ, 16, 128)
    e6b = lambda k: z_copy(k, s9, r9, 3)
    start(NZ, e6b)
    r9[z] = s9[z]
    for a in range(2):
        for b in range(2):
            for p in range(3):
                corr[a, b, p] = fs[a, b + 1, p]
    mid_own = lift[0, t]
    for p in range(3):
        for a in range(2):
            r = p * 4 + a * 2
            corr[a, 0, p, :, pl.ds(0, NC)] = fs[a, 1, p, :, pl.ds(0, NC)] + mid_own[r : r + 2]
    arrive(NZ, e6b)
    back = r9[...].reshape(NC, 128).astype(F32).T
    total = jnp.zeros((64, NC), F32)
    for p in range(3):
        part = dot_nt(back[p * 16 : p * 16 + 16].astype(BF16), leg[p, pl.ds(0, NC), :])
        keep = m0s[p, pl.ds(6, 1), pl.ds(0, NC)]
        diff = dot(wmix[pl.ds(208, 16), :], part * keep, HIGHEST) - oldp[p]
        total += dot(wmix[pl.ds(16 + p * 64, 64), :], diff * changes[p][2], HIGHEST)
    s10[...] = total.astype(BF16).reshape(NT, 16, NC)
    e7 = lambda k: scatter_copy(k, s10, r10, 3)
    start(NT, e7)
    r10[t] = s10[t]
    arrive(NT, e7)
    end_own = lift[1, t] + ((r10[0].astype(F32) + r10[1].astype(F32)) + (r10[2].astype(F32) + r10[3].astype(F32)))
    for p in range(3):
        for a in range(2):
            r = p * 4 + a * 2
            corr[a, 1, p, :, pl.ds(0, NC)] = fs[a, 2, p, :, pl.ds(0, NC)] + end_own[r : r + 2]
    for make in (e1, e4, e4t, e7):
        sent(NT, make)
    for make in (e2a, e3b, e5a, e6b):
        sent(NZ, make)
    for make in (e2b, e3a, e5b, e6a):
        sent(ND, make)


def per_device(fine_state, fold_pairs, legendre, gauss_weights, grid_coef, modes_from, modes_to, mode_rates):
    fine_table, coarse_table = tables()
    sels = selectors()
    fs = jnp.transpose(fine_state, (0, 1, 3, 2, 4))
    leg = jnp.transpose(legendre, (0, 2, 1))
    fold_col = fold_pairs.reshape(NZ, ND, 3).transpose(2, 1, 0).reshape(NC, 1)
    vm = pl.BlockSpec(memory_space=pltpu.VMEM)
    sm = pl.BlockSpec(memory_space=pltpu.SMEM)
    hbm = pl.BlockSpec(memory_space=pl.ANY)
    v = pltpu.VMEM
    dma = pltpu.SemaphoreType.DMA
    scratch = [
        v((3, ROWS, NC), BF16), v((2, 768, HALF), BF16), v((2, 768, CHALF), BF16),
        v((3, 16, ROWS), F32), v((NT, 3, 16, ROWS), BF16), v((3, 16, ROWS), F32), v((3, 16, ROWS), F32),
        v((768, 768), BF16), v((128, 128), BF16), v((128, 128), BF16),
        v((32, NLON), F32), v((32, NLON // 2), F32), v((96, 64), F32), v((224, 16), F32),
        v((NZ, 48, 384), BF16), v((NZ, 48, 384), BF16), v((ND, 80, 128), F32),
        v((ND, 80, 128), BF16), v((ND, 80, 128), BF16), v((ND, 80, 128), BF16), v((ND, 80, 128), BF16),
        v((NZ, 48, 384), BF16), v((NZ, 48, 384), BF16),
        v((NT, 3, 32, NC), BF16), v((NT, 3, 16, ROWS), BF16), v((NT, 3, 16, ROWS), BF16),
        v((3, 48, NC), F32), v((3, 16, NC), F32), v((2, NT, 16, NC), F32),
        v((NZ, 48, 128), BF16), v((NZ, 48, 128), BF16), v((ND, 32, 128), F32),
        v((ND, 32, 128), BF16), v((ND, 32, 128), BF16), v((ND, 32, 128), BF16), v((ND, 32, 128), BF16),
        v((NZ, 48, 128), BF16), v((NZ, 48, 128), BF16), v((NT, 16, NC), BF16), v((NT, 16, NC), BF16),
        dma((3,)), dma((4, NZ)), dma((4, NZ)), dma((4, ND)), dma((4, ND)),
        dma((4, NT)), dma((4, NT)),
    ]
    corr, tend = pl.pallas_call(
        kernel,
        out_shape=(
            jax.ShapeDtypeStruct((2, 2, 3, 2, ROWS), F32),
            jax.ShapeDtypeStruct((2, 3, 3, 2, ROWS), F32),
        ),
        in_specs=[vm, hbm, sm, vm, sm, sm, vm, vm, vm, hbm, hbm] + [vm] * 6,
        out_specs=(vm, vm),
        scratch_shapes=scratch,
        compiler_params=pltpu.CompilerParams(
            collective_id=0, has_side_effects=True, vmem_limit_bytes=48 * 1024 * 1024
        ),
        name="sweep",
    )(
        fs, leg, fold_pairs, fold_col, gauss_weights, mode_rates, grid_coef, modes_to, modes_from,
        jnp.asarray(fine_table), jnp.asarray(coarse_table), *[jnp.asarray(s) for s in sels],
    )
    return (jnp.transpose(corr, (0, 1, 3, 2, 4)), jnp.transpose(tend, (0, 1, 3, 2, 4)))


def solution(mesh):
    placed = (
        P("lev", None, None, "wave", None),
        P(),
        P("wave", "lev", None),
        P("lev"),
        P(),
        P(),
        P(),
        P(),
    )
    return jax.shard_map(
        per_device,
        mesh=mesh,
        in_specs=placed,
        out_specs=(P("lev", None, None, "wave", None), P("lev", None, None, "wave", None)),
        check_vma=False,
    )
```

time: 524 us -> 122 us (0.23); the launches traced: 517 us -> 121 us
  waiting for transfers between devices: 258 us -> 0 us
  Pallas kernels: 0 us -> 105 us
  starting transfers between devices: 71.6 us -> 0 us
  other arithmetic: 55 us -> 0 us
  local copies, waits for them, and re-layouts: 61.6 us -> 15.4 us
  blocking collectives: 29.4 us -> 0 us
  matrix products: 25.9 us -> 0 us
  between operations: 15.2 us -> 0.68 us
    unnamed x8 -> x0, waiting for transfers between devices: 191 us -> none
    pallas_call x0 -> x1, Pallas kernels: none -> 105 us  [per_device(): pl.pallas_call(kernel, out_shape=(jax.ShapeDtypeStruct((2, 2, 3, 2, ROWS)...]
    all_to_all x6 -> x0, starting transfers between devices: 71.5 us -> none  [the longest x2 25.1 us: coarse_eval(): lax.all_to_all(coarse_start(modes), 'wave', split_axis=5, concat_axis=3,...]
    all_to_all x6 -> x0, waiting for transfers between devices: 66.4 us -> none  [the longest x2 36.4 us: coarse_eval(): lax.all_to_all(coarse_grid_step(fourier), 'wave', split_axis=3, concat_ax...]
    another operation x3 -> x0, other arithmetic: 46.9 us -> none
    all_gather x3 -> x0, blocking collectives: 29.4 us -> none  [the longest x2 18.9 us: coarse_start(): gathered = lax.all_gather(modes, 'lev', axis=0, tiled=True)]
    dot_general x16 -> x0, matrix products: 25.9 us -> none  [the longest x3 9.64 us: grid_step(): jnp.einsum('abzk,cpmk->abcpmz', product, wave_table, preferred_element_ty...]
    convert_element_type x7 -> x0, local copies, waits for them, and re-layouts: 25.3 us -> none  [the longest x3 12.7 us: legendre_inverse(): return jnp.einsum('abcpmr,plr->abcpml', split_spec, legendre_table, prefe...]
  transfers between devices with their start and end apart: 10 -> 0, of which waited for: 9 -> 0; matrix products, arithmetic and copies ran while one was open for 13% -> 0% of each run, Pallas kernels for 0% -> 0%
where the time goes in v1:
time: 122 us; the launch traced here: 121 us
  Pallas kernels  105 us (86%)
  local copies, waits for them, and re-layouts  15.4 us (13%)
    pallas_call x1, Pallas kernels, per_device(): pl.pallas_call(kernel, out_shape=(jax.ShapeDtypeStruct((2, 2, 3, 2, ROWS)...  105 us
    unnamed x32, local copies, waits for them, and re-layouts  14.2 us

profile of v1, /device:TPU:1, one launch (start us, length us, event | category | flops | bytes accessed | tf_op | source)
XLA Modules:
  0.0 120.8 jit_solution(3113199943869076601)
XLA Ops:
  0.6 0.9 reshape.10
  1.5 0.2 copy.18
  1.7 0.1 reshape.12.fold_col
  1.8 0.0 copy-start
  1.8 1.5 %copy-done = bf16[2,768,640]{2,1,0:T(8,128)(2,1)S(1)} copy-done((bf16[2,768,640]{2,1,0:T(8,128)(2,1)S(1)}, bf16[2,768,640]{2,1,0:T(8,128)(2,1)}, u32[]{:S(2)}) %copy-start) | copy-done | bytes 1966104
  3.4 0.0 copy-start.1
  3.4 1.5 %copy-done.1 = bf16[3,384,769]{1,2,0:T(8,128)(2,1)S(1)} copy-done((bf16[3,384,769]{1,2,0:T(8,128)(2,1)S(1)}, bf16[3,384,769]{1,2,0:T(8,128)(2,1)}, u32[]{:S(2)}) %copy-start.1) | copy-done | bytes 1771800
  4.9 0.0 copy-start.2
  4.9 0.9 copy-done.2
  5.8 0.0 copy-start.3
  5.8 0.9 copy-done.3
  6.7 0.0 copy-start.4
  6.7 0.9 copy-done.4
  7.5 0.0 copy-start.5
  7.6 0.9 copy-done.5
  8.4 0.0 copy-start.6
  8.4 0.8 copy-done.6
  9.2 0.0 copy-start.7
  9.2 0.8 copy-done.7
  10.0 0.0 copy-start.8
  10.0 0.7 copy-done.8
  10.7 0.0 copy-start.9
  10.7 0.7 copy-done.9
  11.4 0.0 copy-start.10
  11.4 0.7 copy-done.10
  12.1 0.0 copy-start.11
  12.1 0.7 copy-done.11
  12.8 0.0 copy-start.12
  12.8 0.7 copy-done.12
  13.5 0.0 copy-start.13
  13.5 0.7 copy-done.13
  14.1 0.0 copy-start.14
  14.2 0.7 copy-done.14
  14.8 104.7 %sweep.1 = (f32[2,2,3,2,769]{4,3,2,1,0:T(2,128)S(1)}, f32[2,3,3,2,769]{4,3,2,1,0:T(2,128)S(1)}) custom-call(f32[2,3,3,2,769]{4,3,2,1,0:T(2,128)S(1)} %bitcast.7, bf16[3,769,384]{2,1,0:T(8,128)(2,1)S(1)} %bitcast.5, s32[384]{0:T(512)S(1)} %copy-done.8, s32[384,1]{1,0:T(8,128)S(1)} %reshape.12.fold_col, f32[384]{0:T(512)S(1)} %copy-done.13, f32[8]{0:T(128)S(1)} %copy-done.14, ...), custom_call_target="tpu_custom_call" | custom-call | tf_op jit(solution)/shard_map/sweep/pallas_call | solution.py:486
  119.6 0.6 copy.22
  120.2 0.7 copy.23
Async XLA Ops:
  1.8 1.5 %copy-start = (bf16[2,768,640]{2,1,0:T(8,128)(2,1)S(1)}, bf16[2,768,640]{2,1,0:T(8,128)(2,1)}, u32[]{:S(2)}) copy-start(bf16[2,768,640]{2,1,0:T(8,128)(2,1)} %constant.17.clone.tc_hbm) | copy-start | bytes 5898244
  3.4 1.5 %copy-start.1 = (bf16[3,384,769]{1,2,0:T(8,128)(2,1)S(1)}, bf16[3,384,769]{1,2,0:T(8,128)(2,1)}, u32[]{:S(2)}) copy-start(bf16[3,384,769]{1,2,0:T(8,128)(2,1)} %param.18) | copy-start | bytes 5315332
  4.9 0.9 copy-start.2
  5.8 0.9 copy-start.3
  6.7 0.9 copy-start.4
  7.5 0.9 copy-start.5
  8.4 0.8 copy-start.6
  9.2 0.8 copy-start.7
  10.0 0.7 copy-start.8
  10.7 0.7 copy-start.9
  11.4 0.7 copy-start.10
  12.1 0.7 copy-start.11
  12.8 0.7 copy-start.12
  13.5 0.7 copy-start.13
  14.1 0.7 copy-start.14

commit v2 on v1

v2 whole, which is shorter than its diff:
```python
import functools
import math

import jax
import jax.numpy as jnp
import ml_dtypes
import numpy as np
from jax import lax
from jax.experimental import pallas as pl
from jax.experimental.pallas import tpu as pltpu
from jax.sharding import PartitionSpec as P

F32 = jnp.float32
BF16 = jnp.bfloat16
HIGHEST = lax.Precision.HIGHEST
MESH = pl.DeviceIdType.MESH

NLON, LEV, WAVES, ROWS, NC = 2560, 8, 768, 769, 384
HALF, CHALF = NLON // 2, NLON // 4
NZ, ND, NT = 8, 16, 4
FACTOR = 2.0 * WAVES / NLON
QUAD = ((5.0 / 24.0, 1.0 / 3.0, -1.0 / 24.0), (-1.0 / 24.0, 1.0 / 3.0, 5.0 / 24.0))


def table(waves, points, amplitude, count):
    turns = np.outer(waves, np.arange(count)) % points
    angles = turns * (2.0 * math.pi / points)
    return np.concatenate([np.cos(angles), -np.sin(angles)], 0).reshape(2, len(waves), count) * amplitude


def tables():
    t = np.arange(192)
    fine, coarse = [], []
    for parity in (0, 1):
        low = 2 * t + parity
        high = (WAVES - 2 - 2 * t) + parity
        fine.append(table(np.concatenate([low, high]), NLON, WAVES**-0.5, HALF).reshape(768, HALF))
        coarse.append(table(low, NLON // 2, NC**-0.5, CHALF).reshape(NC, CHALF))
    as_bf16 = lambda parts: np.stack(parts).astype(np.float32).astype(ml_dtypes.bfloat16)
    return as_bf16(fine), as_bf16(coarse)


def selectors():
    to_rows = np.zeros((80, 8), np.float32)
    to_mask = np.zeros((80, 64), np.float32)
    to_cols = np.zeros((8, 64), np.float32)
    for lev in range(4):
        for c in range(2):
            for rho in range(8):
                col = lev * 16 + c * 8 + rho
                to_cols[lev * 2 + rho % 2, col] = 1
                node = rho // 2
                for q in range(8):
                    if node < 3:
                        to_mask[node * 16 + c * 8 + q, col] = 1
                        to_mask[48 + c * 8 + q, col] = QUAD[0][node]
                        to_mask[64 + c * 8 + q, col] = QUAD[1][node]
    for row in range(80):
        to_rows[row, row % 8] = 1
    mix_cols = np.zeros((8, 16), np.float32)
    mix_rows = np.zeros((208, 8), np.float32)
    mix_mask = np.zeros((208, 16), np.float32)
    for c in range(2):
        for q in range(8):
            mix_cols[q, c * 8 + q] = 1
            for a in range(8):
                mix_rows[c * 8 + a, a] = 1
                mix_mask[c * 8 + a, c * 8 + q] = 1
                for p in range(3):
                    row = 16 + p * 64 + (a // 2) * 16 + p * 4 + (a % 2) * 2 + c
                    mix_rows[row, a] = 1
                    mix_mask[row, c * 8 + q] = 1
    return to_rows, to_mask, to_cols, mix_rows, mix_mask, mix_cols


def dot(a, b, precision=None):
    return lax.dot_general(a, b, (((1,), (0,)), ((), ())), precision=precision, preferred_element_type=F32)


def dot_nt(a, b):
    return lax.dot_general(a, b, (((1,), (1,)), ((), ())), preferred_element_type=F32)


def kernel(
    fs_hbm, leg_hbm, fold_hbm, gauss_hbm, rates_hbm, coef_hbm, mto_hbm, mfrom_hbm, tf_hbm, tc_hbm,
    to_rows_hbm, to_mask_hbm, to_cols_hbm, mix_rows_hbm, mix_mask_hbm, mix_cols_hbm,
    corr, tend_out,
    fs, fold_s, fold_v, gauss_s, rates_s, coef, mto, mfrom,
    to_rows, to_mask, to_cols, mix_rows, mix_mask, mix_cols,
    leg, tf, tc, xf, gat, m0s, m1s, onehot, perm, permt, coefx, ccoef, wto, wmix, states, parts, oldback, lift, xold,
    stage, stageb, cstage,
    s1a, r1a, s2a, r2a, s1b, r1b, s2b, r2b, s3a, r3a, s4a, r4a, s3b, r3b, s4b, r4b,
    vbuf, s5, r5, s6, r6, s7, r7, s8, r8, s9, r9, s10, r10,
    load_sem, z_send, z_recv, d_send, d_recv, lev_send, lev_recv,
):
    w = lax.axis_index("wave")
    t = lax.axis_index("lev")
    z, d = w // ND, w % ND

    pairs = (
        (leg_hbm, leg), (tf_hbm, tf), (tc_hbm, tc), (fs_hbm, fs), (fold_hbm, fold_s), (fold_hbm, fold_v),
        (gauss_hbm, gauss_s), (rates_hbm, rates_s), (coef_hbm, coef), (mto_hbm, mto), (mfrom_hbm, mfrom),
        (to_rows_hbm, to_rows), (to_mask_hbm, to_mask), (to_cols_hbm, to_cols), (mix_rows_hbm, mix_rows),
        (mix_mask_hbm, mix_mask), (mix_cols_hbm, mix_cols),
    )
    loads = [pltpu.make_async_copy(src, dst, load_sem.at[n]) for n, (src, dst) in enumerate(pairs)]
    for n in (3, 4, 5, 0) + tuple(range(6, 17)) + (1, 2):
        loads[n].start()

    barrier = pltpu.get_barrier_semaphore()

    def lev_dev(k):
        return {"lev": lax.rem(t + k, NT)}

    def z_dev(k):
        return {"wave": lax.rem(z + k, NZ) * ND + d}

    def d_dev(k):
        return {"wave": z * ND + lax.rem(d + k, ND)}

    groups = ((NT, lev_dev), (NZ, z_dev), (ND, d_dev))
    for count, dev in groups:
        @pl.loop(1, count)
        def _(k):
            pl.semaphore_signal(barrier, inc=1, device_id=dev(k), device_id_type=MESH)

    def lev_copy(k, src, dst, row):
        return pltpu.make_async_remote_copy(
            src_ref=src, dst_ref=dst, send_sem=lev_send.at[row, k], recv_sem=lev_recv.at[row, k],
            device_id=lev_dev(k), device_id_type=MESH)

    def z_copy(k, src, dst, row):
        return pltpu.make_async_remote_copy(
            src_ref=src.at[lax.rem(z + k, NZ)], dst_ref=dst.at[z], send_sem=z_send.at[row, k],
            recv_sem=z_recv.at[row, k], device_id=z_dev(k), device_id_type=MESH)

    def d_copy(k, src, dst, row):
        return pltpu.make_async_remote_copy(
            src_ref=src.at[lax.rem(d + k, ND)], dst_ref=dst.at[d], send_sem=d_send.at[row, k],
            recv_sem=d_recv.at[row, k], device_id=d_dev(k), device_id_type=MESH)

    def gather_copy(k, buf, row):
        return lev_copy(k, buf.at[t], buf.at[t], row)

    def scatter_copy(k, src, dst, row):
        return lev_copy(k, src.at[lax.rem(t + k, NT)], dst.at[t], row)

    def start(count, make):
        @pl.loop(1, count)
        def _(k):
            make(k).start()

    def arrive(count, make):
        @pl.loop(1, count)
        def _(k):
            make(k).wait_recv()

    def sent(count, make):
        @pl.loop(1, count)
        def _(k):
            make(k).wait_send()

    loads[3].wait()
    for p in range(3):
        for c in range(2):
            for a in range(2):
                for b in range(3):
                    xf[p, pl.ds(c * 8 + b * 2 + a, 1), :] = fs[a, b, p, pl.ds(c, 1), :]
                xf[p, pl.ds(c * 8 + 6 + a, 1), :] = fs[a, 1, p, pl.ds(c, 1), :]
    gat[t] = xf[...].astype(BF16)
    pl.semaphore_wait(barrier, (NT - 1) + (NZ - 1) + (ND - 1))
    e1 = lambda k: gather_copy(k, gat, 0)
    start(NT, e1)

    for n in range(4, 17):
        loads[n].wait()
    folds = [fold_s[w * 3 + p] for p in range(3)]
    rho = lax.rem(lax.broadcasted_iota(jnp.int32, (16, ROWS), 0), 8)
    row_r = lax.broadcasted_iota(jnp.int32, (16, ROWS), 1)
    for p in range(3):
        first = jnp.where(row_r < WAVES - folds[p], 1.0, 0.0)
        keep = jnp.where(row_r < NC - folds[p], 1.0, 0.0)
        m0s[p] = jnp.where(rho < 6, first, keep)
        m1s[p] = jnp.where(rho < 6, 1.0 - first, 0.0)
    pr = lax.broadcasted_iota(jnp.int32, (128, 128), 0)
    pc = lax.broadcasted_iota(jnp.int32, (128, 128), 1)
    perm[...] = jnp.where(pc == lax.rem(pr, NZ) * ND + pr // NZ, 1.0, 0.0).astype(BF16)
    permt[...] = jnp.where(pr == lax.rem(pc, NZ) * ND + pc // NZ, 1.0, 0.0).astype(BF16)
    stageb[:, pl.ds(24, 8), :] = jnp.zeros((ND, 8, 128), F32)
    arrive(NT, e1)
    loads[0].wait()

    def inverse(p):
        x = gat[:, p].reshape(64, ROWS)
        k0 = jnp.concatenate([m0s[p].astype(BF16)] * 4, 0)
        k1 = jnp.concatenate([m1s[p].astype(BF16)] * 4, 0)
        return dot(jnp.concatenate([x * k0, x * k1], 0), leg[p]).T.reshape(NZ, 48, 128)

    for p in range(2):
        s1a[:, :, pl.ds(p * 128, 128)] = inverse(p).astype(BF16)
    e2az = lambda k: z_copy(k, s1a, r1a, 0)
    start(NZ, e2az)
    r1a[z] = s1a[z]
    f = inverse(2).astype(BF16)
    for j in range(3):
        o = dot(perm[...], f[:, j * 16 : j * 16 + 16].reshape(128, 128))
        stageb[:, pl.ds(j * 8, 8), :] = o.reshape(ND, 8, 128)
    s1b[...] = stageb[...].astype(BF16)
    e2bd = lambda k: d_copy(k, s1b, r1b, 0)
    start(ND, e2bd)
    r1b[d] = s1b[d]

    sr = lax.broadcasted_iota(jnp.int32, (NC, NC), 0)
    sc = lax.broadcasted_iota(jnp.int32, (NC, NC), 1)
    slot_of = (lax.rem(sc, NZ) * ND + lax.rem(sc, 128) // NZ) * 3 + sc // 128
    to_order = jnp.where(sr == slot_of, 1.0, 0.0)
    fold = dot(jnp.broadcast_to(fold_v[...].reshape(1, NC).astype(F32), (8, NC)), to_order, HIGHEST)[:1]
    fold = (fold + 0.5).astype(jnp.int32)
    half_fold, odd = fold // 2, lax.rem(fold, 2)
    rows_n = lax.broadcasted_iota(jnp.int32, (2 * NC, NC), 0)
    onehot[:, pl.ds(0, NC)] = jnp.where(rows_n == 192 + half_fold + NC * (1 - odd), 1.0, 0.0).astype(BF16)
    onehot[:, pl.ds(NC, NC)] = jnp.where(rows_n == half_fold + NC * odd, 1.0, 0.0).astype(BF16)
    onehot[:, pl.ds(2 * NC, NC)] = jnp.where(rows_n == 192 + half_fold + NC * odd, 1.0, 0.0).astype(BF16)

    arrive(NZ, e2az)
    for j in range(3):
        o = dot(perm[...], r1a[:, pl.ds(j * 16, 16), :].reshape(128, 256))
        for p in range(2):
            stage[:, pl.ds(j * 16 + p * 8, 8), :] = o[:, p * 128 : p * 128 + 128].reshape(ND, 8, 128)
    s2a[...] = stage[...].astype(BF16)
    e2ad = lambda k: d_copy(k, s2a, r2a, 1)
    start(ND, e2ad)
    r2a[d] = s2a[d]
    arrive(ND, e2bd)
    stageb[...] = r1b[...].astype(F32)
    for j in range(3):
        x = stageb[:, pl.ds(j * 8, 8), :].reshape(128, 128).astype(BF16)
        s2b[:, pl.ds(j * 16, 16), :] = dot(permt[...], x).astype(BF16).reshape(NZ, 16, 128)
    e2bz = lambda k: z_copy(k, s2b, r2b, 1)
    start(NZ, e2bz)
    r2b[z] = s2b[z]

    for lev in range(NT):
        for n in range(4):
            coefx[pl.ds(lev * 8 + n * 2, 2), :] = coef[pl.ds(lev * 2, 2), :]
    sel_r = lax.broadcasted_iota(jnp.int32, (256, 128), 0)
    sel_c = lax.broadcasted_iota(jnp.int32, (256, 128), 1)
    even = jnp.where(sel_r == 2 * sel_c, 1.0, 0.0)
    chunks = jnp.concatenate([coef[:, pl.ds(n * 256, 256)] for n in range(10)], 0)
    picked = dot(chunks, even, HIGHEST)
    ccoef[...] = jnp.concatenate([picked[n * 8 : n * 8 + 8] for n in range(10)], 1)
    weights = [gauss_s[z * 48 + j * 16 + d] * FACTOR for j in range(3)]
    loads[1].wait()
    loads[2].wait()
    arrive(NZ, e2bz)
    arrive(ND, e2ad)

    stage[...] = r2a[...].astype(F32)
    turned = []
    for j in range(3):
        by_p = [stage[:, pl.ds(j * 16 + p * 8, 8), :].reshape(128, 128) for p in range(2)]
        by_p.append(dot(perm[...], r2b[:, pl.ds(j * 16, 16), :].reshape(128, 128)))
        turned.append(jnp.concatenate(by_p, 0).T)
    natural = []
    for c in range(2):
        rows = []
        for j in range(3):
            members = []
            for i in (1, 0):
                at = [i * 64 + lev * 16 + c * 8 for lev in range(NT)]
                members.append(jnp.concatenate([turned[j][r : r + 8] for r in at], 0))
            rows.append(jnp.concatenate(members, 1))
            for lev in range(NT):
                r = lev * 16 + c * 8 + 6
                xold[pl.ds(j * 8 + lev * 2, 2), pl.ds(c * NC, NC)] = turned[j][r : r + 2]
        x = jnp.concatenate(rows, 0).astype(BF16)
        natural.append(dot_nt(x, onehot[:, pl.ds(0, 2 * NC)]).astype(BF16))

    def grid(x_even, x_odd, tab, c_low, c_high):
        e = dot(x_even, tab[0])
        o = dot(x_odd, tab[1])
        low, high = e + o, e - o
        prod = jnp.concatenate([c_low * low * low, c_high * high * high], 0).astype(BF16)
        n = low.shape[0]
        back_e = dot_nt(prod, tab[0])
        back_o = dot_nt(prod, tab[1])
        return back_e[:n] + back_e[n:], back_o[:n] - back_o[n:]

    x_even = jnp.concatenate([n[:, :NC] for n in natural], 1)
    x_odd = jnp.concatenate([n[:, NC:] for n in natural], 1)
    fe, fo = grid(
        x_even, x_odd, tf,
        jnp.concatenate([coefx[:, pl.ds(0, HALF)]] * 3, 0), jnp.concatenate([coefx[:, pl.ds(HALF, HALF)]] * 3, 0),
    )
    row = lax.broadcasted_iota(jnp.int32, (96, 1), 0)
    wt = jnp.where(row < 32, weights[0], jnp.where(row < 64, weights[1], weights[2]))
    wt = jnp.where(lax.rem(row, 8) < 6, wt, 0.0)
    be = (fe * wt).astype(BF16)
    bo = (fo * wt).astype(BF16)
    slot = []
    for c in range(2):
        y = jnp.concatenate([be[:, c * NC : c * NC + NC], bo[:, c * NC : c * NC + NC]], 1)
        slot.append(dot(y, onehot[:, pl.ds(0, 2 * NC)]))
    for j in range(3):
        pieces = []
        for i in range(2):
            for lev in range(NT):
                for c in range(2):
                    r = j * 32 + lev * 8
                    pieces.append(slot[c][r : r + 8, (1 - i) * NC : (2 - i) * NC])
        back = jnp.concatenate(pieces, 0).T
        for p in range(2):
            stage[:, pl.ds(j * 16 + p * 8, 8), :] = back[p * 128 : p * 128 + 128].reshape(ND, 8, 128)
        o = dot(permt[...], back[256:].astype(BF16))
        s3b[:, pl.ds(j * 16, 16), :] = o.astype(BF16).reshape(NZ, 16, 128)
    s3a[...] = stage[...].astype(BF16)
    e3ad = lambda k: d_copy(k, s3a, r3a, 2)
    e3bz = lambda k: z_copy(k, s3b, r3b, 2)
    start(ND, e3ad)
    start(NZ, e3bz)
    r3a[d] = s3a[d]
    r3b[z] = s3b[z]

    row = lax.broadcasted_iota(jnp.int32, (32, 1), 0)
    wt_c = jnp.where(row < 8, weights[0], jnp.where(row < 16, weights[1], weights[2]))

    def coarse_grid(x):
        n = dot_nt(x, onehot[:, pl.ds(NC, 2 * NC)]).astype(BF16)
        ge, go = grid(
            n[:, :NC], n[:, NC:], tc,
            jnp.concatenate([ccoef[:, pl.ds(0, CHALF)]] * 4, 0), jnp.concatenate([ccoef[:, pl.ds(CHALF, CHALF)]] * 4, 0),
        )
        return jnp.concatenate([ge * wt_c, go * wt_c], 1)

    xold[pl.ds(24, 8), :] = jnp.zeros((8, 2 * NC), F32)
    oldback[...] = coarse_grid(xold[...].astype(BF16))

    arrive(ND, e3ad)
    stage[...] = r3a[...].astype(F32)
    for j in range(3):
        by_p = [stage[:, pl.ds(j * 16 + p * 8, 8), :].reshape(128, 128) for p in range(2)]
        o = dot(permt[...], jnp.concatenate(by_p, 1).astype(BF16))
        s4a[:, pl.ds(j * 16, 16), :] = o.astype(BF16).reshape(NZ, 16, 256)
    e3az = lambda k: z_copy(k, s4a, r4a, 3)
    start(NZ, e3az)
    r4a[z] = s4a[z]
    arrive(NZ, e3bz)
    for j in range(3):
        o = dot(perm[...], r3b[:, pl.ds(j * 16, 16), :].reshape(128, 128))
        stageb[:, pl.ds(j * 8, 8), :] = o.reshape(ND, 8, 128)
    s4b[...] = stageb[...].astype(BF16)
    e3bd = lambda k: d_copy(k, s4b, r4b, 3)
    start(ND, e3bd)
    r4b[d] = s4b[d]

    wto[...] = dot(dot(to_rows[...], mto[...], HIGHEST), to_cols[...], HIGHEST) * to_mask[...]
    wmix[pl.ds(0, 208), :] = dot(dot(mix_rows[...], mfrom[...], HIGHEST), mix_cols[...], HIGHEST) * mix_mask[...]
    wmix[pl.ds(208, 16), :] = (
        dot(dot(mix_rows[pl.ds(0, 16), :], mto[...], HIGHEST), mix_cols[...], HIGHEST) * mix_mask[pl.ds(0, 16), :]
    )
    keeps = [m0s[p, pl.ds(6, 1), pl.ds(0, NC)] for p in range(3)]
    for p in range(3):
        x = gat[:, p, :, pl.ds(0, NC)].reshape(64, NC).astype(F32)
        states[p] = dot(wto[pl.ds(0, 48), :], x, HIGHEST) * keeps[p]

    def forward(p, x):
        o = dot_nt(x.T.astype(BF16), leg[p])
        k0 = jnp.concatenate([m0s[p]] * 4, 0)
        k1 = jnp.concatenate([m1s[p]] * 4, 0)
        part = o[:64] * k0 + o[64:] * k1
        parts[p] = part
        vbuf[t, p] = dot(wto[pl.ds(48, 32), :], part[:, :NC] * keeps[p], HIGHEST).astype(BF16)

    arrive(ND, e3bd)
    stageb[...] = r4b[...].astype(F32)
    pieces = []
    for j in range(3):
        x = stageb[:, pl.ds(j * 8, 8), :].reshape(128, 128).astype(BF16)
        pieces.append(dot(permt[...], x).reshape(NZ, 16, 128))
    forward(2, jnp.concatenate(pieces, 1).reshape(NC, 128))
    arrive(NZ, e3az)
    for p in range(2):
        forward(p, r4a[:, :, pl.ds(p * 128, 128)].reshape(NC, 128).astype(F32))
    e4 = lambda k: gather_copy(k, vbuf, 1)
    start(NT, e4)
    for p in range(3):
        s5[:, p] = parts[p].astype(BF16).reshape(NT, 16, ROWS)

    mode = lax.rem(lax.broadcasted_iota(jnp.int32, (16, NC), 0), 8)
    rate = jnp.zeros((16, NC), F32)
    for q in range(8):
        rate = jnp.where(mode == q, rates_s[q], rate)
    col = lax.broadcasted_iota(jnp.int32, (16, NC), 1)
    known = []
    for p in range(3):
        degree = (col + folds[p]).astype(F32)
        stiff = rate * (degree * (degree + 1.0) / (NC * (NC + 1.0)))
        old = [states[p, pl.ds(b * 16, 16), :] for b in range(3)]
        int_mid = stiff * (QUAD[0][0] * old[0] + QUAD[0][1] * old[1] + QUAD[0][2] * old[2])
        int_end = stiff * (QUAD[1][0] * old[0] + QUAD[1][1] * old[1] + QUAD[1][2] * old[2])
        inv = 1.0 / (1.0 + 0.5 * stiff)
        known.append((inv, old[0] + 0.5 * stiff * old[1] - int_mid, 0.5 * stiff * old[2] - int_end, old[1], old[2]))
    arrive(NT, e4)
    e4t = lambda k: scatter_copy(k, s5, r5, 2)
    start(NT, e4t)
    r5[t] = s5[t]
    fourier, changes = [], []
    for p in range(3):
        inv, known_mid, known_end, old_1, old_2 = known[p]
        tend = (vbuf[0, p].astype(F32) + vbuf[1, p].astype(F32)) + (vbuf[2, p].astype(F32) + vbuf[3, p].astype(F32))
        mid = (known_mid + tend[:16]) * inv
        levels = (dot(wmix[pl.ds(0, 16), :], mid, HIGHEST) * keeps[p]).astype(BF16)
        fourier.append(dot(levels, leg[p, pl.ds(0, NC), :]))
        changes.append((mid - old_1, (mid + known_end + tend[16:]) * inv - old_2, 0.5 * inv))
    rest = jnp.zeros((80, NC), F32)
    f = jnp.concatenate(fourier + [rest], 0).T.reshape(NZ, 48, 128)
    s6[:, pl.ds(0, 16), :] = (f[:, :16] + pltpu.roll(f[:, 16:32], 64, 2)).astype(BF16)
    s6[:, pl.ds(16, 16), :] = f[:, 32:].astype(BF16)
    e5a = lambda k: z_copy(k, s6, r6, 4)
    start(NZ, e5a)
    r6[z] = s6[z]
    lifted_mid = jnp.zeros((64, NC), F32)
    lifted_end = jnp.zeros((64, NC), F32)
    for p in range(3):
        place = wmix[pl.ds(16 + p * 64, 64), :]
        lifted_mid += dot(place, changes[p][0], HIGHEST)
        lifted_end += dot(place, changes[p][1], HIGHEST)
    lift[0] = lifted_mid.reshape(NT, 16, NC)
    lift[1] = lifted_end.reshape(NT, 16, NC)
    arrive(NZ, e5a)
    for h in range(2):
        o = dot(perm[...], r6[:, pl.ds(h * 16, 16), :].reshape(128, 128))
        cstage[:, pl.ds(h * 8, 8), :] = o.reshape(ND, 8, 128)
    s7[...] = cstage[...].astype(BF16)
    e5b = lambda k: d_copy(k, s7, r7, 4)
    start(ND, e5b)
    r7[d] = s7[d]
    arrive(NT, e4t)
    for p in range(3):
        total = (r5[0, p].astype(F32) + r5[1, p].astype(F32)) + (r5[2, p].astype(F32) + r5[3, p].astype(F32))
        for c in range(2):
            for a in range(2):
                for b in range(3):
                    r = c * 8 + b * 2 + a
                    tend_out[a, b, p, pl.ds(c, 1), :] = total[r : r + 1]
    arrive(ND, e5b)

    cstage[...] = r7[...].astype(F32)
    turned = [cstage[:, pl.ds(h * 8, 8), :].reshape(128, 128).T for h in range(2)]
    at_j = ((0, 0), (0, 64), (1, 0))
    rows = []
    for h, first_row in at_j:
        at = [first_row + p * 16 + c * 8 for c in range(2) for p in range(3)]
        rows.append(jnp.concatenate([turned[h][r : r + 8] for r in at], 1))
    rows.append(jnp.zeros((8, 2 * NC), F32))
    fresh = coarse_grid(jnp.concatenate(rows, 0).astype(BF16))
    slot = dot((fresh - oldback[...]).astype(BF16), onehot[:, pl.ds(NC, 2 * NC)])
    by_j = []
    for j in range(3):
        by_j.append([slot[j * 8 : j * 8 + 8, c * NC + p * 128 : c * NC + p * 128 + 128] for p in range(3) for c in range(2)])
    gap = [jnp.zeros((16, 128), F32)]
    for h, group in enumerate((by_j[0] + gap + by_j[1] + gap, by_j[2] + gap * 5)):
        cstage[:, pl.ds(h * 8, 8), :] = jnp.concatenate(group, 0).T.reshape(ND, 8, 128)
    s8[...] = cstage[...].astype(BF16)
    e6a = lambda k: d_copy(k, s8, r8, 5)
    start(ND, e6a)
    r8[d] = s8[d]
    for a in range(2):
        for b in range(2):
            for p in range(3):
                corr[a, b, p] = fs[a, b + 1, p]
    mid_own = lift[0, t]
    for p in range(3):
        for a in range(2):
            r = p * 4 + a * 2
            corr[a, 0, p, :, pl.ds(0, NC)] = fs[a, 1, p, :, pl.ds(0, NC)] + mid_own[r : r + 2]
    arrive(ND, e6a)
    cstage[...] = r8[...].astype(F32)
    for h in range(2):
        x = cstage[:, pl.ds(h * 8, 8), :].reshape(128, 128).astype(BF16)
        s9[:, pl.ds(h * 16, 16), :] = dot(permt[...], x).astype(BF16).reshape(NZ, 16, 128)
    e6b = lambda k: z_copy(k, s9, r9, 5)
    start(NZ, e6b)
    r9[z] = s9[z]
    arrive(NZ, e6b)
    x = r9[...].astype(F32)
    back = jnp.concatenate([x[:, :16], pltpu.roll(x[:, :16], 64, 2), x[:, 16:]], 1).reshape(NC, 128).T
    total = jnp.zeros((64, NC), F32)
    for p in range(3):
        part = dot_nt(back[p * 16 : p * 16 + 16].astype(BF16), leg[p, pl.ds(0, NC), :])
        diff = dot(wmix[pl.ds(208, 16), :], part * keeps[p], HIGHEST)
        total += dot(wmix[pl.ds(16 + p * 64, 64), :], diff * changes[p][2], HIGHEST)
    s10[...] = total.astype(BF16).reshape(NT, 16, NC)
    e7 = lambda k: scatter_copy(k, s10, r10, 3)
    start(NT, e7)
    r10[t] = s10[t]
    arrive(NT, e7)
    end_own = lift[1, t] + ((r10[0].astype(F32) + r10[1].astype(F32)) + (r10[2].astype(F32) + r10[3].astype(F32)))
    for p in range(3):
        for a in range(2):
            r = p * 4 + a * 2
            corr[a, 1, p, :, pl.ds(0, NC)] = fs[a, 2, p, :, pl.ds(0, NC)] + end_own[r : r + 2]
    for make in (e1, e4, e4t, e7):
        sent(NT, make)
    for make in (e2az, e2bz, e3bz, e3az, e5a, e6b):
        sent(NZ, make)
    for make in (e2bd, e2ad, e3ad, e3bd, e5b, e6a):
        sent(ND, make)


def per_device(fine_state, fold_pairs, legendre, gauss_weights, grid_coef, modes_from, modes_to, mode_rates):
    fine_table, coarse_table = tables()
    sels = selectors()
    fs = jnp.transpose(fine_state, (0, 1, 3, 2, 4))
    leg = jnp.transpose(legendre, (0, 2, 1))
    vm = pl.BlockSpec(memory_space=pltpu.VMEM)
    hbm = pl.BlockSpec(memory_space=pltpu.HBM)
    v, sm = pltpu.VMEM, pltpu.SMEM
    dma = pltpu.SemaphoreType.DMA
    scratch = [
        v((2, 3, 3, 2, ROWS), F32), sm((NC,), jnp.int32), v((NC,), jnp.int32), sm((NC,), F32), sm((LEV,), F32),
        v((LEV, NLON), F32), v((8, 8), F32), v((8, 8), F32), v((80, 8), F32), v((80, 64), F32), v((8, 64), F32),
        v((208, 8), F32), v((208, 16), F32), v((8, 16), F32),
        v((3, ROWS, NC), BF16), v((2, 768, HALF), BF16), v((2, NC, CHALF), BF16),
        v((3, 16, ROWS), F32), v((NT, 3, 16, ROWS), BF16), v((3, 16, ROWS), F32), v((3, 16, ROWS), F32),
        v((768, 3 * NC), BF16), v((128, 128), BF16), v((128, 128), BF16),
        v((32, NLON), F32), v((LEV, NLON // 2), F32), v((80, 64), F32), v((224, 16), F32),
        v((3, 48, NC), F32), v((3, 64, ROWS), F32), v((32, 768), F32), v((2, NT, 16, NC), F32), v((32, 768), F32),
        v((ND, 48, 128), F32), v((ND, 32, 128), F32), v((ND, 16, 128), F32),
    ]
    z_two, z_one = v((NZ, 48, 256), BF16), v((NZ, 48, 128), BF16)
    d_two, d_one = v((ND, 48, 128), BF16), v((ND, 32, 128), BF16)
    scratch += [z_two, z_two, d_two, d_two, d_one, d_one, z_one, z_one]
    scratch += [d_two, d_two, z_two, z_two, z_one, z_one, d_one, d_one]
    scratch += [v((NT, 3, 32, NC), BF16), v((NT, 3, 16, ROWS), BF16), v((NT, 3, 16, ROWS), BF16)]
    z_coarse, d_coarse, lev_coarse = v((NZ, 32, 128), BF16), v((ND, 16, 128), BF16), v((NT, 16, NC), BF16)
    scratch += [z_coarse] * 2 + [d_coarse] * 4 + [z_coarse] * 2 + [lev_coarse] * 2
    scratch += [
        dma((17,)), dma((6, NZ)), dma((6, NZ)), dma((6, ND)), dma((6, ND)), dma((4, NT)), dma((4, NT)),
    ]
    corr, tend = pl.pallas_call(
        kernel,
        out_shape=(
            jax.ShapeDtypeStruct((2, 2, 3, 2, ROWS), F32),
            jax.ShapeDtypeStruct((2, 3, 3, 2, ROWS), F32),
        ),
        in_specs=[hbm] * 16,
        out_specs=(vm, vm),
        scratch_shapes=scratch,
        compiler_params=pltpu.CompilerParams(
            collective_id=0, has_side_effects=True, vmem_limit_bytes=64 * 1024 * 1024
        ),
        name="sweep",
    )(
        fs, leg, fold_pairs, gauss_weights, mode_rates, grid_coef, modes_to, modes_from,
        jnp.asarray(fine_table), jnp.asarray(coarse_table), *[jnp.asarray(s) for s in sels],
    )
    return (jnp.transpose(corr, (0, 1, 3, 2, 4)), jnp.transpose(tend, (0, 1, 3, 2, 4)))


def solution(mesh):
    placed = (
        P("lev", None, None, "wave", None),
        P(),
        P("wave", "lev", None),
        P("lev"),
        P(),
        P(),
        P(),
        P(),
    )
    return jax.shard_map(
        per_device,
        mesh=mesh,
        in_specs=placed,
        out_specs=(P("lev", None, None, "wave", None), P("lev", None, None, "wave", None)),
        check_vma=False,
    )
```

time: 122 us -> 96 us (0.79)
  Pallas kernels: 105 us -> 91.3 us
  local copies, waits for them, and re-layouts: 15.4 us -> 3.11 us
    pallas_call x1, Pallas kernels: 105 us -> 91.3 us  [per_device(): pl.pallas_call(kernel, out_shape=(jax.ShapeDtypeStruct((2, 2, 3, 2, ROWS)...]
    unnamed x32 -> x2, local copies, waits for them, and re-layouts: 14.2 us -> 3.11 us
where the time goes in v2:
time: 96 us; the launch traced here: 95 us
  Pallas kernels  91.3 us (95%)
  local copies, waits for them, and re-layouts  3.11 us (3%)
    pallas_call x1, Pallas kernels, per_device(): pl.pallas_call(kernel, out_shape=(jax.ShapeDtypeStruct((2, 2, 3, 2, ROWS)...  91.3 us
    unnamed x2, local copies, waits for them, and re-layouts  3.11 us

profile of v2, /device:TPU:1, one launch (start us, length us, event | category | flops | bytes accessed | tf_op | source)
XLA Modules:
  0.0 95.0 jit_solution(9579938777879743715)
XLA Ops:
  0.6 91.3 %sweep.1 = (f32[2,2,3,2,769]{4,3,2,1,0:T(2,128)}, f32[2,3,3,2,769]{4,3,2,1,0:T(2,128)}) custom-call(f32[2,3,3,2,769]{4,3,2,1,0:T(2,128)} %bitcast.5, bf16[3,769,384]{2,1,0:T(8,128)(2,1)} %bitcast.4, s32[384]{0:T(512)} %fold_hbm.1, f32[384]{0:T(512)} %gauss_hbm.1, f32[8]{0:T(128)} %rates_hbm.1, f32[8,2560]{1,0:T(8,128)} %coef_hbm.1, f32[8,8]{1,0:T(8,128)} %mto_hbm.1, ...), custom_call_target="tpu_custom_call" | custom-call | tf_op jit(solution)/shard_map/sweep/pallas_call | solution.py:541
  91.9 1.5 %copy.20 = f32[2,2,2,3,769]{4,2,3,1,0:T(2,128)} copy(f32[2,2,2,3,769]{4,2,3,1,0:T(2,128)} %bitcast.7) | data formatting | bytes 147648
  93.5 1.6 %copy.21 = f32[2,3,2,3,769]{4,2,3,1,0:T(2,128)} copy(f32[2,3,2,3,769]{4,2,3,1,0:T(2,128)} %bitcast.6) | data formatting | bytes 221472

commit v3 on v2

--- a/solution.py
+++ b/solution.py
@@ -16,7 +16,7 @@
 MESH = pl.DeviceIdType.MESH
 
 NLON, LEV, WAVES, ROWS, NC = 2560, 8, 768, 769, 384
-HALF, CHALF = NLON // 2, NLON // 4
+HALF, CLON = NLON // 2, NLON // 2
 NZ, ND, NT = 8, 16, 4
 FACTOR = 2.0 * WAVES / NLON
 QUAD = ((5.0 / 24.0, 1.0 / 3.0, -1.0 / 24.0), (-1.0 / 24.0, 1.0 / 3.0, 5.0 / 24.0))
@@ -30,14 +30,14 @@
 
 def tables():
     t = np.arange(192)
-    fine, coarse = [], []
+    fine = []
     for parity in (0, 1):
         low = 2 * t + parity
         high = (WAVES - 2 - 2 * t) + parity
         fine.append(table(np.concatenate([low, high]), NLON, WAVES**-0.5, HALF).reshape(768, HALF))
-        coarse.append(table(low, NLON // 2, NC**-0.5, CHALF).reshape(NC, CHALF))
-    as_bf16 = lambda parts: np.stack(parts).astype(np.float32).astype(ml_dtypes.bfloat16)
-    return as_bf16(fine), as_bf16(coarse)
+    coarse = table(np.arange(NC), NLON // 2, NC**-0.5, NLON // 2)
+    as_bf16 = lambda values: values.astype(np.float32).astype(ml_dtypes.bfloat16)
+    return as_bf16(np.stack(fine)), as_bf16(coarse)
 
 
 def selectors():
@@ -57,19 +57,20 @@
                         to_mask[64 + c * 8 + q, col] = QUAD[1][node]
     for row in range(80):
         to_rows[row, row % 8] = 1
-    mix_cols = np.zeros((8, 16), np.float32)
-    mix_rows = np.zeros((208, 8), np.float32)
-    mix_mask = np.zeros((208, 16), np.float32)
+    mix_cols = np.zeros((8, 48), np.float32)
+    mix_rows = np.zeros((80, 8), np.float32)
+    mix_mask = np.zeros((80, 48), np.float32)
     for c in range(2):
         for q in range(8):
-            mix_cols[q, c * 8 + q] = 1
+            for p in range(3):
+                mix_cols[q, p * 16 + c * 8 + q] = 1
             for a in range(8):
                 mix_rows[c * 8 + a, a] = 1
                 mix_mask[c * 8 + a, c * 8 + q] = 1
                 for p in range(3):
-                    row = 16 + p * 64 + (a // 2) * 16 + p * 4 + (a % 2) * 2 + c
+                    row = 16 + (a // 2) * 16 + p * 4 + (a % 2) * 2 + c
                     mix_rows[row, a] = 1
-                    mix_mask[row, c * 8 + q] = 1
+                    mix_mask[row, p * 16 + c * 8 + q] = 1
     return to_rows, to_mask, to_cols, mix_rows, mix_mask, mix_cols
 
 
@@ -87,10 +88,10 @@
     corr, tend_out,
     fs, fold_s, fold_v, gauss_s, rates_s, coef, mto, mfrom,
     to_rows, to_mask, to_cols, mix_rows, mix_mask, mix_cols,
-    leg, tf, tc, xf, gat, m0s, m1s, onehot, perm, permt, coefx, ccoef, wto, wmix, states, parts, oldback, lift, xold,
+    leg, tf, tc, xf, gat, m0s, m1s, onehot, ordered, tslot, perm, permt, coefx, ccoef, wto, wmix, wplace, states, parts, oldback, lift, xold,
     stage, stageb, cstage,
     s1a, r1a, s2a, r2a, s1b, r1b, s2b, r2b, s3a, r3a, s4a, r4a, s3b, r3b, s4b, r4b,
-    vbuf, s5, r5, s6, r6, s7, r7, s8, r8, s9, r9, s10, r10,
+    vmid, vend, s5, r5, s6, r6, s7, r7, s8, r8, s9, r9, s10, r10,
     load_sem, z_send, z_recv, d_send, d_recv, lev_send, lev_recv,
 ):
     w = lax.axis_index("wave")
@@ -167,10 +168,12 @@
                 for b in range(3):
                     xf[p, pl.ds(c * 8 + b * 2 + a, 1), :] = fs[a, b, p, pl.ds(c, 1), :]
                 xf[p, pl.ds(c * 8 + 6 + a, 1), :] = fs[a, 1, p, pl.ds(c, 1), :]
-    gat[t] = xf[...].astype(BF16)
+    for p in range(3):
+        gat[p, t] = xf[p].astype(BF16)
     pl.semaphore_wait(barrier, (NT - 1) + (NZ - 1) + (ND - 1))
-    e1 = lambda k: gather_copy(k, gat, 0)
-    start(NT, e1)
+    e1 = [lambda k, p=p: gather_copy(k, gat.at[p], 5 + p) for p in range(3)]
+    for p in (2, 0, 1):
+        start(NT, e1[p])
 
     for n in range(4, 17):
         loads[n].wait()
@@ -187,20 +190,15 @@
     perm[...] = jnp.where(pc == lax.rem(pr, NZ) * ND + pr // NZ, 1.0, 0.0).astype(BF16)
     permt[...] = jnp.where(pr == lax.rem(pc, NZ) * ND + pc // NZ, 1.0, 0.0).astype(BF16)
     stageb[:, pl.ds(24, 8), :] = jnp.zeros((ND, 8, 128), F32)
-    arrive(NT, e1)
     loads[0].wait()
 
     def inverse(p):
-        x = gat[:, p].reshape(64, ROWS)
+        arrive(NT, e1[p])
+        x = gat[p].reshape(64, ROWS)
         k0 = jnp.concatenate([m0s[p].astype(BF16)] * 4, 0)
         k1 = jnp.concatenate([m1s[p].astype(BF16)] * 4, 0)
         return dot(jnp.concatenate([x * k0, x * k1], 0), leg[p]).T.reshape(NZ, 48, 128)
 
-    for p in range(2):
-        s1a[:, :, pl.ds(p * 128, 128)] = inverse(p).astype(BF16)
-    e2az = lambda k: z_copy(k, s1a, r1a, 0)
-    start(NZ, e2az)
-    r1a[z] = s1a[z]
     f = inverse(2).astype(BF16)
     for j in range(3):
         o = dot(perm[...], f[:, j * 16 : j * 16 + 16].reshape(128, 128))
@@ -209,6 +207,12 @@
     e2bd = lambda k: d_copy(k, s1b, r1b, 0)
     start(ND, e2bd)
     r1b[d] = s1b[d]
+
+    for p in range(2):
+        s1a[:, :, pl.ds(p * 128, 128)] = inverse(p).astype(BF16)
+    e2az = lambda k: z_copy(k, s1a, r1a, 0)
+    start(NZ, e2az)
+    r1a[z] = s1a[z]
 
     sr = lax.broadcasted_iota(jnp.int32, (NC, NC), 0)
     sc = lax.broadcasted_iota(jnp.int32, (NC, NC), 1)
@@ -218,9 +222,9 @@
     fold = (fold + 0.5).astype(jnp.int32)
     half_fold, odd = fold // 2, lax.rem(fold, 2)
     rows_n = lax.broadcasted_iota(jnp.int32, (2 * NC, NC), 0)
-    onehot[:, pl.ds(0, NC)] = jnp.where(rows_n == 192 + half_fold + NC * (1 - odd), 1.0, 0.0).astype(BF16)
-    onehot[:, pl.ds(NC, NC)] = jnp.where(rows_n == half_fold + NC * odd, 1.0, 0.0).astype(BF16)
-    onehot[:, pl.ds(2 * NC, NC)] = jnp.where(rows_n == 192 + half_fold + NC * odd, 1.0, 0.0).astype(BF16)
+    onehot[:, pl.ds(0, NC)] = jnp.where(rows_n == half_fold + NC * odd, 1.0, 0.0).astype(BF16)
+    onehot[:, pl.ds(NC, NC)] = jnp.where(rows_n == 192 + half_fold + NC * (1 - odd), 1.0, 0.0).astype(BF16)
+    ordered[...] = jnp.where(sr == fold, 1.0, 0.0).T.astype(BF16)
 
     arrive(NZ, e2az)
     for j in range(3):
@@ -266,7 +270,7 @@
         rows = []
         for j in range(3):
             members = []
-            for i in (1, 0):
+            for i in range(2):
                 at = [i * 64 + lev * 16 + c * 8 for lev in range(NT)]
                 members.append(jnp.concatenate([turned[j][r : r + 8] for r in at], 0))
             rows.append(jnp.concatenate(members, 1))
@@ -274,7 +278,7 @@
                 r = lev * 16 + c * 8 + 6
                 xold[pl.ds(j * 8 + lev * 2, 2), pl.ds(c * NC, NC)] = turned[j][r : r + 2]
         x = jnp.concatenate(rows, 0).astype(BF16)
-        natural.append(dot_nt(x, onehot[:, pl.ds(0, 2 * NC)]).astype(BF16))
+        natural.append(dot_nt(x, onehot[...]).astype(BF16))
 
     def grid(x_even, x_odd, tab, c_low, c_high):
         e = dot(x_even, tab[0])
@@ -300,14 +304,14 @@
     slot = []
     for c in range(2):
         y = jnp.concatenate([be[:, c * NC : c * NC + NC], bo[:, c * NC : c * NC + NC]], 1)
-        slot.append(dot(y, onehot[:, pl.ds(0, 2 * NC)]))
+        slot.append(dot(y, onehot[...]))
     for j in range(3):
         pieces = []
         for i in range(2):
             for lev in range(NT):
                 for c in range(2):
                     r = j * 32 + lev * 8
-                    pieces.append(slot[c][r : r + 8, (1 - i) * NC : (2 - i) * NC])
+                    pieces.append(slot[c][r : r + 8, i * NC : i * NC + NC])
         back = jnp.concatenate(pieces, 0).T
         for p in range(2):
             stage[:, pl.ds(j * 16 + p * 8, 8), :] = back[p * 128 : p * 128 + 128].reshape(ND, 8, 128)
@@ -325,13 +329,12 @@
     wt_c = jnp.where(row < 8, weights[0], jnp.where(row < 16, weights[1], weights[2]))
 
     def coarse_grid(x):
-        n = dot_nt(x, onehot[:, pl.ds(NC, 2 * NC)]).astype(BF16)
-        ge, go = grid(
-            n[:, :NC], n[:, NC:], tc,
-            jnp.concatenate([ccoef[:, pl.ds(0, CHALF)]] * 4, 0), jnp.concatenate([ccoef[:, pl.ds(CHALF, CHALF)]] * 4, 0),
-        )
-        return jnp.concatenate([ge * wt_c, go * wt_c], 1)
-
+        g = dot(x, tslot[...])
+        prod = (jnp.concatenate([ccoef[...]] * 4, 0) * g * g).astype(BF16)
+        return dot_nt(prod, tslot[...]) * wt_c
+
+    for c in range(2):
+        tslot[pl.ds(c * NC, NC), :] = dot(ordered[...], tc[c]).astype(BF16)
     xold[pl.ds(24, 8), :] = jnp.zeros((8, 2 * NC), F32)
     oldback[...] = coarse_grid(xold[...].astype(BF16))
 
@@ -354,13 +357,14 @@
     r4b[d] = s4b[d]
 
     wto[...] = dot(dot(to_rows[...], mto[...], HIGHEST), to_cols[...], HIGHEST) * to_mask[...]
-    wmix[pl.ds(0, 208), :] = dot(dot(mix_rows[...], mfrom[...], HIGHEST), mix_cols[...], HIGHEST) * mix_mask[...]
-    wmix[pl.ds(208, 16), :] = (
-        dot(dot(mix_rows[pl.ds(0, 16), :], mto[...], HIGHEST), mix_cols[...], HIGHEST) * mix_mask[pl.ds(0, 16), :]
-    )
+    mixed = dot(dot(mix_rows[...], mfrom[...], HIGHEST), mix_cols[...], HIGHEST) * mix_mask[...]
+    wmix[pl.ds(0, 16), :] = mixed[:16, :16]
+    wplace[...] = mixed[16:]
+    mixed = dot(dot(mix_rows[pl.ds(0, 16), :], mto[...], HIGHEST), mix_cols[...], HIGHEST) * mix_mask[pl.ds(0, 16), :]
+    wmix[pl.ds(16, 16), :] = mixed[:, :16]
     keeps = [m0s[p, pl.ds(6, 1), pl.ds(0, NC)] for p in range(3)]
     for p in range(3):
-        x = gat[:, p, :, pl.ds(0, NC)].reshape(64, NC).astype(F32)
+        x = gat[p, :, :, pl.ds(0, NC)].reshape(64, NC).astype(F32)
         states[p] = dot(wto[pl.ds(0, 48), :], x, HIGHEST) * keeps[p]
 
     def forward(p, x):
@@ -369,7 +373,9 @@
         k1 = jnp.concatenate([m1s[p]] * 4, 0)
         part = o[:64] * k0 + o[64:] * k1
         parts[p] = part
-        vbuf[t, p] = dot(wto[pl.ds(48, 32), :], part[:, :NC] * keeps[p], HIGHEST).astype(BF16)
+        mixed = dot(wto[pl.ds(48, 32), :], part[:, :NC] * keeps[p], HIGHEST).astype(BF16)
+        vmid[t, p] = mixed[:16]
+        vend[t, p] = mixed[16:]
 
     arrive(ND, e3bd)
     stageb[...] = r4b[...].astype(F32)
@@ -381,7 +387,7 @@
     arrive(NZ, e3az)
     for p in range(2):
         forward(p, r4a[:, :, pl.ds(p * 128, 128)].reshape(NC, 128).astype(F32))
-    e4 = lambda k: gather_copy(k, vbuf, 1)
+    e4 = lambda k: gather_copy(k, vmid, 1)
     start(NT, e4)
     for p in range(3):
         s5[:, p] = parts[p].astype(BF16).reshape(NT, 16, ROWS)
@@ -401,17 +407,14 @@
         inv = 1.0 / (1.0 + 0.5 * stiff)
         known.append((inv, old[0] + 0.5 * stiff * old[1] - int_mid, 0.5 * stiff * old[2] - int_end, old[1], old[2]))
     arrive(NT, e4)
-    e4t = lambda k: scatter_copy(k, s5, r5, 2)
-    start(NT, e4t)
-    r5[t] = s5[t]
-    fourier, changes = [], []
+    fourier, mids = [], []
     for p in range(3):
         inv, known_mid, known_end, old_1, old_2 = known[p]
-        tend = (vbuf[0, p].astype(F32) + vbuf[1, p].astype(F32)) + (vbuf[2, p].astype(F32) + vbuf[3, p].astype(F32))
-        mid = (known_mid + tend[:16]) * inv
+        tend = (vmid[0, p].astype(F32) + vmid[1, p].astype(F32)) + (vmid[2, p].astype(F32) + vmid[3, p].astype(F32))
+        mid = (known_mid + tend) * inv
         levels = (dot(wmix[pl.ds(0, 16), :], mid, HIGHEST) * keeps[p]).astype(BF16)
         fourier.append(dot(levels, leg[p, pl.ds(0, NC), :]))
-        changes.append((mid - old_1, (mid + known_end + tend[16:]) * inv - old_2, 0.5 * inv))
+        mids.append(mid)
     rest = jnp.zeros((80, NC), F32)
     f = jnp.concatenate(fourier + [rest], 0).T.reshape(NZ, 48, 128)
     s6[:, pl.ds(0, 16), :] = (f[:, :16] + pltpu.roll(f[:, 16:32], 64, 2)).astype(BF16)
@@ -419,14 +422,13 @@
     e5a = lambda k: z_copy(k, s6, r6, 4)
     start(NZ, e5a)
     r6[z] = s6[z]
-    lifted_mid = jnp.zeros((64, NC), F32)
-    lifted_end = jnp.zeros((64, NC), F32)
-    for p in range(3):
-        place = wmix[pl.ds(16 + p * 64, 64), :]
-        lifted_mid += dot(place, changes[p][0], HIGHEST)
-        lifted_end += dot(place, changes[p][1], HIGHEST)
-    lift[0] = lifted_mid.reshape(NT, 16, NC)
-    lift[1] = lifted_end.reshape(NT, 16, NC)
+    e4e = lambda k: gather_copy(k, vend, 4)
+    start(NT, e4e)
+    e4t = lambda k: scatter_copy(k, s5, r5, 2)
+    start(NT, e4t)
+    r5[t] = s5[t]
+    place = wplace[...]
+    lift[0] = dot(place, jnp.concatenate([mids[p] - known[p][3] for p in range(3)], 0), HIGHEST).reshape(NT, 16, NC)
     arrive(NZ, e5a)
     for h in range(2):
         o = dot(perm[...], r6[:, pl.ds(h * 16, 16), :].reshape(128, 128))
@@ -435,14 +437,13 @@
     e5b = lambda k: d_copy(k, s7, r7, 4)
     start(ND, e5b)
     r7[d] = s7[d]
-    arrive(NT, e4t)
-    for p in range(3):
-        total = (r5[0, p].astype(F32) + r5[1, p].astype(F32)) + (r5[2, p].astype(F32) + r5[3, p].astype(F32))
-        for c in range(2):
-            for a in range(2):
-                for b in range(3):
-                    r = c * 8 + b * 2 + a
-                    tend_out[a, b, p, pl.ds(c, 1), :] = total[r : r + 1]
+    arrive(NT, e4e)
+    ends = []
+    for p in range(3):
+        inv, known_mid, known_end, old_1, old_2 = known[p]
+        tend = (vend[0, p].astype(F32) + vend[1, p].astype(F32)) + (vend[2, p].astype(F32) + vend[3, p].astype(F32))
+        ends.append((mids[p] + known_end + tend) * inv - old_2)
+    lift[1] = dot(place, jnp.concatenate(ends, 0), HIGHEST).reshape(NT, 16, NC)
     arrive(ND, e5b)
 
     cstage[...] = r7[...].astype(F32)
@@ -454,7 +455,7 @@
         rows.append(jnp.concatenate([turned[h][r : r + 8] for r in at], 1))
     rows.append(jnp.zeros((8, 2 * NC), F32))
     fresh = coarse_grid(jnp.concatenate(rows, 0).astype(BF16))
-    slot = dot((fresh - oldback[...]).astype(BF16), onehot[:, pl.ds(NC, 2 * NC)])
+    slot = (fresh - oldback[...]).astype(BF16).astype(F32)
     by_j = []
     for j in range(3):
         by_j.append([slot[j * 8 : j * 8 + 8, c * NC + p * 128 : c * NC + p * 128 + 128] for p in range(3) for c in range(2)])
@@ -474,6 +475,20 @@
         for a in range(2):
             r = p * 4 + a * 2
             corr[a, 0, p, :, pl.ds(0, NC)] = fs[a, 1, p, :, pl.ds(0, NC)] + mid_own[r : r + 2]
+    for make in (*e1, e4, e4e, e4t):
+        sent(NT, make)
+    for make in (e2az, e2bz, e3bz, e3az, e5a):
+        sent(NZ, make)
+    for make in (e2bd, e2ad, e3ad, e3bd, e5b):
+        sent(ND, make)
+    arrive(NT, e4t)
+    for p in range(3):
+        total = (r5[0, p].astype(F32) + r5[1, p].astype(F32)) + (r5[2, p].astype(F32) + r5[3, p].astype(F32))
+        for c in range(2):
+            for a in range(2):
+                for b in range(3):
+                    r = c * 8 + b * 2 + a
+                    tend_out[a, b, p, pl.ds(c, 1), :] = total[r : r + 1]
     arrive(ND, e6a)
     cstage[...] = r8[...].astype(F32)
     for h in range(2):
@@ -482,14 +497,16 @@
     e6b = lambda k: z_copy(k, s9, r9, 5)
     start(NZ, e6b)
     r9[z] = s9[z]
+    sent(ND, e6a)
     arrive(NZ, e6b)
     x = r9[...].astype(F32)
     back = jnp.concatenate([x[:, :16], pltpu.roll(x[:, :16], 64, 2), x[:, 16:]], 1).reshape(NC, 128).T
-    total = jnp.zeros((64, NC), F32)
-    for p in range(3):
-        part = dot_nt(back[p * 16 : p * 16 + 16].astype(BF16), leg[p, pl.ds(0, NC), :])
-        diff = dot(wmix[pl.ds(208, 16), :], part * keeps[p], HIGHEST)
-        total += dot(wmix[pl.ds(16 + p * 64, 64), :], diff * changes[p][2], HIGHEST)
+    partial = []
+    for p in range(3):
+        partial.append(dot_nt(back[p * 16 : p * 16 + 16].astype(BF16), leg[p, pl.ds(0, NC), :]) * keeps[p])
+    diff = dot(wmix[pl.ds(16, 16), :], jnp.concatenate(partial, 1), HIGHEST)
+    scaled = [diff[:, p * NC : p * NC + NC] * (0.5 * known[p][0]) for p in range(3)]
+    total = dot(place, jnp.concatenate(scaled, 0), HIGHEST)
     s10[...] = total.astype(BF16).reshape(NT, 16, NC)
     e7 = lambda k: scatter_copy(k, s10, r10, 3)
     start(NT, e7)
@@ -500,12 +517,8 @@
         for a in range(2):
             r = p * 4 + a * 2
             corr[a, 1, p, :, pl.ds(0, NC)] = fs[a, 2, p, :, pl.ds(0, NC)] + end_own[r : r + 2]
-    for make in (e1, e4, e4t, e7):
-        sent(NT, make)
-    for make in (e2az, e2bz, e3bz, e3az, e5a, e6b):
-        sent(NZ, make)
-    for make in (e2bd, e2ad, e3ad, e3bd, e5b, e6a):
-        sent(ND, make)
+    sent(NT, e7)
+    sent(NZ, e6b)
 
 
 def per_device(fine_state, fold_pairs, legendre, gauss_weights, grid_coef, modes_from, modes_to, mode_rates):
@@ -520,11 +533,11 @@
     scratch = [
         v((2, 3, 3, 2, ROWS), F32), sm((NC,), jnp.int32), v((NC,), jnp.int32), sm((NC,), F32), sm((LEV,), F32),
         v((LEV, NLON), F32), v((8, 8), F32), v((8, 8), F32), v((80, 8), F32), v((80, 64), F32), v((8, 64), F32),
-        v((208, 8), F32), v((208, 16), F32), v((8, 16), F32),
-        v((3, ROWS, NC), BF16), v((2, 768, HALF), BF16), v((2, NC, CHALF), BF16),
-        v((3, 16, ROWS), F32), v((NT, 3, 16, ROWS), BF16), v((3, 16, ROWS), F32), v((3, 16, ROWS), F32),
-        v((768, 3 * NC), BF16), v((128, 128), BF16), v((128, 128), BF16),
-        v((32, NLON), F32), v((LEV, NLON // 2), F32), v((80, 64), F32), v((224, 16), F32),
+        v((80, 8), F32), v((80, 48), F32), v((8, 48), F32),
+        v((3, ROWS, NC), BF16), v((2, 768, HALF), BF16), v((2, NC, CLON), BF16),
+        v((3, 16, ROWS), F32), v((3, NT, 16, ROWS), BF16), v((3, 16, ROWS), F32), v((3, 16, ROWS), F32),
+        v((768, 768), BF16), v((NC, NC), BF16), v((768, CLON), BF16), v((128, 128), BF16), v((128, 128), BF16),
+        v((32, NLON), F32), v((LEV, CLON), F32), v((80, 64), F32), v((32, 16), F32), v((64, 48), F32),
         v((3, 48, NC), F32), v((3, 64, ROWS), F32), v((32, 768), F32), v((2, NT, 16, NC), F32), v((32, 768), F32),
         v((ND, 48, 128), F32), v((ND, 32, 128), F32), v((ND, 16, 128), F32),
     ]
@@ -532,11 +545,15 @@
     d_two, d_one = v((ND, 48, 128), BF16), v((ND, 32, 128), BF16)
     scratch += [z_two, z_two, d_two, d_two, d_one, d_one, z_one, z_one]
     scratch += [d_two, d_two, z_two, z_two, z_one, z_one, d_one, d_one]
-    scratch += [v((NT, 3, 32, NC), BF16), v((NT, 3, 16, ROWS), BF16), v((NT, 3, 16, ROWS), BF16)]
+    scratch += [v((NT, 3, 16, NC), BF16), v((NT, 3, 16, NC), BF16), v((NT, 3, 16, ROWS), BF16), v((NT, 3, 16, ROWS), BF16)]
     z_coarse, d_coarse, lev_coarse = v((NZ, 32, 128), BF16), v((ND, 16, 128), BF16), v((NT, 16, NC), BF16)
     scratch += [z_coarse] * 2 + [d_coarse] * 4 + [z_coarse] * 2 + [lev_coarse] * 2
     scratch += [
-        dma((17,)), dma((6, NZ)), dma((6, NZ)), dma((6, ND)), dma((6, ND)), dma((4, NT)), dma((4, NT)),
+        dma((17,)), dma((6, NZ)), dma((6, NZ)), dma((6, ND)), dma((6, ND)), dma((8, NT)), dma((8, NT)),
+    ]
+    operands = [
+        fs, leg, fold_pairs, gauss_weights, mode_rates, grid_coef, modes_to, modes_from,
+        jnp.asarray(fine_table), jnp.asarray(coarse_table), *[jnp.asarray(s) for s in sels],
     ]
     corr, tend = pl.pallas_call(
         kernel,
@@ -548,13 +565,10 @@
         out_specs=(vm, vm),
         scratch_shapes=scratch,
         compiler_params=pltpu.CompilerParams(
-            collective_id=0, has_side_effects=True, vmem_limit_bytes=64 * 1024 * 1024
+            collective_id=0, has_side_effects=True, vmem_limit_bytes=48 * 1024 * 1024
         ),
         name="sweep",
-    )(
-        fs, leg, fold_pairs, gauss_weights, mode_rates, grid_coef, modes_to, modes_from,
-        jnp.asarray(fine_table), jnp.asarray(coarse_table), *[jnp.asarray(s) for s in sels],
-    )
+    )(*[pltpu.with_memory_space_constraint(x, pltpu.HBM) for x in operands])
     return (jnp.transpose(corr, (0, 1, 3, 2, 4)), jnp.transpose(tend, (0, 1, 3, 2, 4)))
 
 

time: 96 us -> 89.6 us (0.933)
  Pallas kernels: 91.3 us -> 87.2 us
  local copies, waits for them, and re-layouts: 3.11 us -> 1.29 us
    pallas_call x1, Pallas kernels: 91.3 us -> 87.2 us  [per_device(): pl.pallas_call(kernel, out_shape=(jax.ShapeDtypeStruct((2, 2, 3, 2, ROWS)...]
    unnamed x2, local copies, waits for them, and re-layouts: 3.11 us -> 1.29 us
where the time goes in v3:
time: 89.6 us; the launch traced here: 89.1 us
  Pallas kernels  87.2 us (97%)
  local copies, waits for them, and re-layouts  1.29 us (1%)
    pallas_call x1, Pallas kernels, per_device(): pl.pallas_call(kernel, out_shape=(jax.ShapeDtypeStruct((2, 2, 3, 2, ROWS)...  87.2 us

profile of v3, /device:TPU:1, one launch (start us, length us, event | category | flops | bytes accessed | tf_op | source)
XLA Modules:
  0.0 89.1 jit_solution(17062814267823338794)
XLA Ops:
  0.6 87.2 %sweep.1 = (f32[2,2,3,2,769]{4,3,2,1,0:T(2,128)S(1)}, f32[2,3,3,2,769]{4,3,2,1,0:T(2,128)S(1)}) custom-call(f32[2,3,3,2,769]{4,3,2,1,0:T(2,128)} %bitcast.7, bf16[3,769,384]{2,1,0:T(8,128)(2,1)} %bitcast.6, s32[384]{0:T(512)} %fold_hbm.1, f32[384]{0:T(512)} %gauss_hbm.1, f32[8]{0:T(128)} %rates_hbm.1, f32[8,2560]{1,0:T(8,128)} %coef_hbm.1, f32[8,8]{1,0:T(8,128)} %mto_hbm.1, ...), custom_call_target="tpu_custom_call" | custom-call | tf_op jit(solution)/shard_map/sweep/pallas_call | solution.py:558
  87.8 0.6 copy.20
  88.4 0.7 copy.21

commit v4 on v3

--- a/solution.py
+++ b/solution.py
@@ -105,8 +105,7 @@
         (mix_mask_hbm, mix_mask), (mix_cols_hbm, mix_cols),
     )
     loads = [pltpu.make_async_copy(src, dst, load_sem.at[n]) for n, (src, dst) in enumerate(pairs)]
-    for n in (3, 4, 5, 0) + tuple(range(6, 17)) + (1, 2):
-        loads[n].start()
+    loads[3].start()
 
     barrier = pltpu.get_barrier_semaphore()
 
@@ -124,6 +123,9 @@
         @pl.loop(1, count)
         def _(k):
             pl.semaphore_signal(barrier, inc=1, device_id=dev(k), device_id_type=MESH)
+
+    for n in (0, 4, 5) + tuple(range(6, 17)) + (1, 2):
+        loads[n].start()
 
     def lev_copy(k, src, dst, row):
         return pltpu.make_async_remote_copy(
@@ -197,9 +199,14 @@
         x = gat[p].reshape(64, ROWS)
         k0 = jnp.concatenate([m0s[p].astype(BF16)] * 4, 0)
         k1 = jnp.concatenate([m1s[p].astype(BF16)] * 4, 0)
-        return dot(jnp.concatenate([x * k0, x * k1], 0), leg[p]).T.reshape(NZ, 48, 128)
-
-    f = inverse(2).astype(BF16)
+        low = pl.ds(0, ROWS - 1)
+        both = jnp.concatenate([(x * k0)[:, : ROWS - 1], (x * k1)[:, : ROWS - 1]], 0)
+        f = dot(both, leg[p, low, :])
+        last = (x * k1)[:, ROWS - 1 :].astype(F32) * leg[p, pl.ds(ROWS - 1, 1), :].astype(F32)
+        f = jnp.concatenate([f[:64], f[64:] + last], 0)
+        return f.astype(BF16).T.reshape(NZ, 48, 128)
+
+    f = inverse(2)
     for j in range(3):
         o = dot(perm[...], f[:, j * 16 : j * 16 + 16].reshape(128, 128))
         stageb[:, pl.ds(j * 8, 8), :] = o.reshape(ND, 8, 128)
@@ -207,12 +214,11 @@
     e2bd = lambda k: d_copy(k, s1b, r1b, 0)
     start(ND, e2bd)
     r1b[d] = s1b[d]
-
+    e2az = [lambda k, p=p: z_copy(k, s1a.at[p], r1a.at[p], p * 6) for p in range(2)]
     for p in range(2):
-        s1a[:, :, pl.ds(p * 128, 128)] = inverse(p).astype(BF16)
-    e2az = lambda k: z_copy(k, s1a, r1a, 0)
-    start(NZ, e2az)
-    r1a[z] = s1a[z]
+        s1a[p] = inverse(p)
+        start(NZ, e2az[p])
+        r1a[p, z] = s1a[p, z]
 
     sr = lax.broadcasted_iota(jnp.int32, (NC, NC), 0)
     sc = lax.broadcasted_iota(jnp.int32, (NC, NC), 1)
@@ -226,11 +232,11 @@
     onehot[:, pl.ds(NC, NC)] = jnp.where(rows_n == 192 + half_fold + NC * (1 - odd), 1.0, 0.0).astype(BF16)
     ordered[...] = jnp.where(sr == fold, 1.0, 0.0).T.astype(BF16)
 
-    arrive(NZ, e2az)
-    for j in range(3):
-        o = dot(perm[...], r1a[:, pl.ds(j * 16, 16), :].reshape(128, 256))
-        for p in range(2):
-            stage[:, pl.ds(j * 16 + p * 8, 8), :] = o[:, p * 128 : p * 128 + 128].reshape(ND, 8, 128)
+    for p in range(2):
+        arrive(NZ, e2az[p])
+        for j in range(3):
+            o = dot(perm[...], r1a[p, :, pl.ds(j * 16, 16), :].reshape(128, 128))
+            stage[:, pl.ds(j * 16 + p * 8, 8), :] = o.reshape(ND, 8, 128)
     s2a[...] = stage[...].astype(BF16)
     e2ad = lambda k: d_copy(k, s2a, r2a, 1)
     start(ND, e2ad)
@@ -265,9 +271,8 @@
         by_p = [stage[:, pl.ds(j * 16 + p * 8, 8), :].reshape(128, 128) for p in range(2)]
         by_p.append(dot(perm[...], r2b[:, pl.ds(j * 16, 16), :].reshape(128, 128)))
         turned.append(jnp.concatenate(by_p, 0).T)
-    natural = []
+    rows = []
     for c in range(2):
-        rows = []
         for j in range(3):
             members = []
             for i in range(2):
@@ -277,8 +282,7 @@
             for lev in range(NT):
                 r = lev * 16 + c * 8 + 6
                 xold[pl.ds(j * 8 + lev * 2, 2), pl.ds(c * NC, NC)] = turned[j][r : r + 2]
-        x = jnp.concatenate(rows, 0).astype(BF16)
-        natural.append(dot_nt(x, onehot[...]).astype(BF16))
+    natural = dot_nt(jnp.concatenate(rows, 0).astype(BF16), onehot[...]).astype(BF16)
 
     def grid(x_even, x_odd, tab, c_low, c_high):
         e = dot(x_even, tab[0])
@@ -290,8 +294,8 @@
         back_o = dot_nt(prod, tab[1])
         return back_e[:n] + back_e[n:], back_o[:n] - back_o[n:]
 
-    x_even = jnp.concatenate([n[:, :NC] for n in natural], 1)
-    x_odd = jnp.concatenate([n[:, NC:] for n in natural], 1)
+    x_even = jnp.concatenate([natural[:96, :NC], natural[96:, :NC]], 1)
+    x_odd = jnp.concatenate([natural[:96, NC:], natural[96:, NC:]], 1)
     fe, fo = grid(
         x_even, x_odd, tf,
         jnp.concatenate([coefx[:, pl.ds(0, HALF)]] * 3, 0), jnp.concatenate([coefx[:, pl.ds(HALF, HALF)]] * 3, 0),
@@ -301,17 +305,15 @@
     wt = jnp.where(lax.rem(row, 8) < 6, wt, 0.0)
     be = (fe * wt).astype(BF16)
     bo = (fo * wt).astype(BF16)
-    slot = []
-    for c in range(2):
-        y = jnp.concatenate([be[:, c * NC : c * NC + NC], bo[:, c * NC : c * NC + NC]], 1)
-        slot.append(dot(y, onehot[...]))
+    y = [jnp.concatenate([be[:, c * NC : c * NC + NC], bo[:, c * NC : c * NC + NC]], 1) for c in range(2)]
+    slot = dot(jnp.concatenate(y, 0), onehot[...])
     for j in range(3):
         pieces = []
         for i in range(2):
             for lev in range(NT):
                 for c in range(2):
-                    r = j * 32 + lev * 8
-                    pieces.append(slot[c][r : r + 8, i * NC : i * NC + NC])
+                    r = c * 96 + j * 32 + lev * 8
+                    pieces.append(slot[r : r + 8, i * NC : i * NC + NC])
         back = jnp.concatenate(pieces, 0).T
         for p in range(2):
             stage[:, pl.ds(j * 16 + p * 8, 8), :] = back[p * 128 : p * 128 + 128].reshape(ND, 8, 128)
@@ -340,13 +342,13 @@
 
     arrive(ND, e3ad)
     stage[...] = r3a[...].astype(F32)
-    for j in range(3):
-        by_p = [stage[:, pl.ds(j * 16 + p * 8, 8), :].reshape(128, 128) for p in range(2)]
-        o = dot(permt[...], jnp.concatenate(by_p, 1).astype(BF16))
-        s4a[:, pl.ds(j * 16, 16), :] = o.astype(BF16).reshape(NZ, 16, 256)
-    e3az = lambda k: z_copy(k, s4a, r4a, 3)
-    start(NZ, e3az)
-    r4a[z] = s4a[z]
+    e3az = [lambda k, p=p: z_copy(k, s4a.at[p], r4a.at[p], 3 + p * 4) for p in range(2)]
+    for p in range(2):
+        for j in range(3):
+            x = stage[:, pl.ds(j * 16 + p * 8, 8), :].reshape(128, 128).astype(BF16)
+            s4a[p, :, pl.ds(j * 16, 16), :] = dot(permt[...], x).astype(BF16).reshape(NZ, 16, 128)
+        start(NZ, e3az[p])
+        r4a[p, z] = s4a[p, z]
     arrive(NZ, e3bz)
     for j in range(3):
         o = dot(perm[...], r3b[:, pl.ds(j * 16, 16), :].reshape(128, 128))
@@ -368,7 +370,7 @@
         states[p] = dot(wto[pl.ds(0, 48), :], x, HIGHEST) * keeps[p]
 
     def forward(p, x):
-        o = dot_nt(x.T.astype(BF16), leg[p])
+        o = dot_nt(x.T, leg[p])
         k0 = jnp.concatenate([m0s[p]] * 4, 0)
         k1 = jnp.concatenate([m1s[p]] * 4, 0)
         part = o[:64] * k0 + o[64:] * k1
@@ -382,11 +384,11 @@
     pieces = []
     for j in range(3):
         x = stageb[:, pl.ds(j * 8, 8), :].reshape(128, 128).astype(BF16)
-        pieces.append(dot(permt[...], x).reshape(NZ, 16, 128))
+        pieces.append(dot(permt[...], x).astype(BF16).reshape(NZ, 16, 128))
     forward(2, jnp.concatenate(pieces, 1).reshape(NC, 128))
-    arrive(NZ, e3az)
     for p in range(2):
-        forward(p, r4a[:, :, pl.ds(p * 128, 128)].reshape(NC, 128).astype(F32))
+        arrive(NZ, e3az[p])
+        forward(p, r4a[p].reshape(NC, 128))
     e4 = lambda k: gather_copy(k, vmid, 1)
     start(NT, e4)
     for p in range(3):
@@ -407,14 +409,15 @@
         inv = 1.0 / (1.0 + 0.5 * stiff)
         known.append((inv, old[0] + 0.5 * stiff * old[1] - int_mid, 0.5 * stiff * old[2] - int_end, old[1], old[2]))
     arrive(NT, e4)
-    fourier, mids = [], []
-    for p in range(3):
-        inv, known_mid, known_end, old_1, old_2 = known[p]
+    mids = []
+    for p in range(3):
         tend = (vmid[0, p].astype(F32) + vmid[1, p].astype(F32)) + (vmid[2, p].astype(F32) + vmid[3, p].astype(F32))
-        mid = (known_mid + tend) * inv
-        levels = (dot(wmix[pl.ds(0, 16), :], mid, HIGHEST) * keeps[p]).astype(BF16)
-        fourier.append(dot(levels, leg[p, pl.ds(0, NC), :]))
-        mids.append(mid)
+        mids.append((known[p][1] + tend) * known[p][0])
+    levels = dot(wmix[pl.ds(0, 16), :], jnp.concatenate(mids, 1), HIGHEST)
+    fourier = []
+    for p in range(3):
+        x = (levels[:, p * NC : p * NC + NC] * keeps[p]).astype(BF16)
+        fourier.append(dot(x, leg[p, pl.ds(0, NC), :]))
     rest = jnp.zeros((80, NC), F32)
     f = jnp.concatenate(fourier + [rest], 0).T.reshape(NZ, 48, 128)
     s6[:, pl.ds(0, 16), :] = (f[:, :16] + pltpu.roll(f[:, 16:32], 64, 2)).astype(BF16)
@@ -477,7 +480,7 @@
             corr[a, 0, p, :, pl.ds(0, NC)] = fs[a, 1, p, :, pl.ds(0, NC)] + mid_own[r : r + 2]
     for make in (*e1, e4, e4e, e4t):
         sent(NT, make)
-    for make in (e2az, e2bz, e3bz, e3az, e5a):
+    for make in (*e2az, e2bz, e3bz, *e3az, e5a):
         sent(NZ, make)
     for make in (e2bd, e2ad, e3ad, e3bd, e5b):
         sent(ND, make)
@@ -541,7 +544,7 @@
         v((3, 48, NC), F32), v((3, 64, ROWS), F32), v((32, 768), F32), v((2, NT, 16, NC), F32), v((32, 768), F32),
         v((ND, 48, 128), F32), v((ND, 32, 128), F32), v((ND, 16, 128), F32),
     ]
-    z_two, z_one = v((NZ, 48, 256), BF16), v((NZ, 48, 128), BF16)
+    z_two, z_one = v((2, NZ, 48, 128), BF16), v((NZ, 48, 128), BF16)
     d_two, d_one = v((ND, 48, 128), BF16), v((ND, 32, 128), BF16)
     scratch += [z_two, z_two, d_two, d_two, d_one, d_one, z_one, z_one]
     scratch += [d_two, d_two, z_two, z_two, z_one, z_one, d_one, d_one]
@@ -549,7 +552,7 @@
     z_coarse, d_coarse, lev_coarse = v((NZ, 32, 128), BF16), v((ND, 16, 128), BF16), v((NT, 16, NC), BF16)
     scratch += [z_coarse] * 2 + [d_coarse] * 4 + [z_coarse] * 2 + [lev_coarse] * 2
     scratch += [
-        dma((17,)), dma((6, NZ)), dma((6, NZ)), dma((6, ND)), dma((6, ND)), dma((8, NT)), dma((8, NT)),
+        dma((17,)), dma((8, NZ)), dma((8, NZ)), dma((6, ND)), dma((6, ND)), dma((8, NT)), dma((8, NT)),
     ]
     operands = [
         fs, leg, fold_pairs, gauss_weights, mode_rates, grid_coef, modes_to, modes_from,

time: 89.6 us -> 88.5 us (0.988)
  no operation moved by 1% of the time
where the time goes in v4:
time: 88.5 us; the launch traced here: 88.4 us
  Pallas kernels  86.5 us (98%)
  local copies, waits for them, and re-layouts  1.29 us (1%)
    pallas_call x1, Pallas kernels, per_device(): pl.pallas_call(kernel, out_shape=(jax.ShapeDtypeStruct((2, 2, 3, 2, ROWS)...  86.5 us

profile of v4, /device:TPU:1, one launch (start us, length us, event | category | flops | bytes accessed | tf_op | source)
XLA Modules:
  0.0 88.4 jit_solution(12139600092268110025)
XLA Ops:
  0.6 86.5 %sweep.1 = (f32[2,2,3,2,769]{4,3,2,1,0:T(2,128)S(1)}, f32[2,3,3,2,769]{4,3,2,1,0:T(2,128)S(1)}) custom-call(f32[2,3,3,2,769]{4,3,2,1,0:T(2,128)} %bitcast.7, bf16[3,769,384]{2,1,0:T(8,128)(2,1)} %bitcast.6, s32[384]{0:T(512)} %fold_hbm.1, f32[384]{0:T(512)} %gauss_hbm.1, f32[8]{0:T(128)} %rates_hbm.1, f32[8,2560]{1,0:T(8,128)} %coef_hbm.1, f32[8,8]{1,0:T(8,128)} %mto_hbm.1, ...), custom_call_target="tpu_custom_call" | custom-call | tf_op jit(solution)/shard_map/sweep/pallas_call | solution.py:561
  87.1 0.6 copy.20
  87.8 0.7 copy.21

commit v5 on v4

--- a/solution.py
+++ b/solution.py
@@ -262,6 +262,8 @@
     weights = [gauss_s[z * 48 + j * 16 + d] * FACTOR for j in range(3)]
     loads[1].wait()
     loads[2].wait()
+    for c in range(2):
+        tslot[pl.ds(c * NC, NC), :] = dot(ordered[...], tc[c]).astype(BF16)
     arrive(NZ, e2bz)
     arrive(ND, e2ad)
 
@@ -335,8 +337,6 @@
         prod = (jnp.concatenate([ccoef[...]] * 4, 0) * g * g).astype(BF16)
         return dot_nt(prod, tslot[...]) * wt_c
 
-    for c in range(2):
-        tslot[pl.ds(c * NC, NC), :] = dot(ordered[...], tc[c]).astype(BF16)
     xold[pl.ds(24, 8), :] = jnp.zeros((8, 2 * NC), F32)
     oldback[...] = coarse_grid(xold[...].astype(BF16))
 

time: 88.5 us -> 88.5 us (level)
  no operation moved by 1% of the time
where the time goes in v5:
time: 88.5 us; the launch traced here: 88.4 us
  Pallas kernels  86.5 us (98%)
  local copies, waits for them, and re-layouts  1.29 us (1%)
    pallas_call x1, Pallas kernels, per_device(): pl.pallas_call(kernel, out_shape=(jax.ShapeDtypeStruct((2, 2, 3, 2, ROWS)...  86.5 us

profile of v5, /device:TPU:1, one launch (start us, length us, event | category | flops | bytes accessed | tf_op | source)
XLA Modules:
  0.0 88.4 jit_solution(1984992780020025849)
XLA Ops:
  0.6 86.5 %sweep.1 = (f32[2,2,3,2,769]{4,3,2,1,0:T(2,128)S(1)}, f32[2,3,3,2,769]{4,3,2,1,0:T(2,128)S(1)}) custom-call(f32[2,3,3,2,769]{4,3,2,1,0:T(2,128)} %bitcast.7, bf16[3,769,384]{2,1,0:T(8,128)(2,1)} %bitcast.6, s32[384]{0:T(512)} %fold_hbm.1, f32[384]{0:T(512)} %gauss_hbm.1, f32[8]{0:T(128)} %rates_hbm.1, f32[8,2560]{1,0:T(8,128)} %coef_hbm.1, f32[8,8]{1,0:T(8,128)} %mto_hbm.1, ...), custom_call_target="tpu_custom_call" | custom-call | tf_op jit(solution)/shard_map/sweep/pallas_call | solution.py:561
  87.1 0.6 copy.20
  87.8 0.7 copy.21

commit v6 on v4

--- a/solution.py
+++ b/solution.py
@@ -369,6 +369,8 @@
         x = gat[p, :, :, pl.ds(0, NC)].reshape(64, NC).astype(F32)
         states[p] = dot(wto[pl.ds(0, 48), :], x, HIGHEST) * keeps[p]
 
+    e4 = [lambda k, p=p: gather_copy(k, vmid.at[p], 8 + p) for p in range(3)]
+
     def forward(p, x):
         o = dot_nt(x.T, leg[p])
         k0 = jnp.concatenate([m0s[p]] * 4, 0)
@@ -376,8 +378,9 @@
         part = o[:64] * k0 + o[64:] * k1
         parts[p] = part
         mixed = dot(wto[pl.ds(48, 32), :], part[:, :NC] * keeps[p], HIGHEST).astype(BF16)
-        vmid[t, p] = mixed[:16]
+        vmid[p, t] = mixed[:16]
         vend[t, p] = mixed[16:]
+        start(NT, e4[p])
 
     arrive(ND, e3bd)
     stageb[...] = r4b[...].astype(F32)
@@ -389,8 +392,6 @@
     for p in range(2):
         arrive(NZ, e3az[p])
         forward(p, r4a[p].reshape(NC, 128))
-    e4 = lambda k: gather_copy(k, vmid, 1)
-    start(NT, e4)
     for p in range(3):
         s5[:, p] = parts[p].astype(BF16).reshape(NT, 16, ROWS)
 
@@ -408,10 +409,11 @@
         int_end = stiff * (QUAD[1][0] * old[0] + QUAD[1][1] * old[1] + QUAD[1][2] * old[2])
         inv = 1.0 / (1.0 + 0.5 * stiff)
         known.append((inv, old[0] + 0.5 * stiff * old[1] - int_mid, 0.5 * stiff * old[2] - int_end, old[1], old[2]))
-    arrive(NT, e4)
+    for p in range(3):
+        arrive(NT, e4[p])
     mids = []
     for p in range(3):
-        tend = (vmid[0, p].astype(F32) + vmid[1, p].astype(F32)) + (vmid[2, p].astype(F32) + vmid[3, p].astype(F32))
+        tend = (vmid[p, 0].astype(F32) + vmid[p, 1].astype(F32)) + (vmid[p, 2].astype(F32) + vmid[p, 3].astype(F32))
         mids.append((known[p][1] + tend) * known[p][0])
     levels = dot(wmix[pl.ds(0, 16), :], jnp.concatenate(mids, 1), HIGHEST)
     fourier = []
@@ -478,7 +480,7 @@
         for a in range(2):
             r = p * 4 + a * 2
             corr[a, 0, p, :, pl.ds(0, NC)] = fs[a, 1, p, :, pl.ds(0, NC)] + mid_own[r : r + 2]
-    for make in (*e1, e4, e4e, e4t):
+    for make in (*e1, *e4, e4e, e4t):
         sent(NT, make)
     for make in (*e2az, e2bz, e3bz, *e3az, e5a):
         sent(NZ, make)
@@ -548,11 +550,11 @@
     d_two, d_one = v((ND, 48, 128), BF16), v((ND, 32, 128), BF16)
     scratch += [z_two, z_two, d_two, d_two, d_one, d_one, z_one, z_one]
     scratch += [d_two, d_two, z_two, z_two, z_one, z_one, d_one, d_one]
-    scratch += [v((NT, 3, 16, NC), BF16), v((NT, 3, 16, NC), BF16), v((NT, 3, 16, ROWS), BF16), v((NT, 3, 16, ROWS), BF16)]
+    scratch += [v((3, NT, 16, NC), BF16), v((NT, 3, 16, NC), BF16), v((NT, 3, 16, ROWS), BF16), v((NT, 3, 16, ROWS), BF16)]
     z_coarse, d_coarse, lev_coarse = v((NZ, 32, 128), BF16), v((ND, 16, 128), BF16), v((NT, 16, NC), BF16)
     scratch += [z_coarse] * 2 + [d_coarse] * 4 + [z_coarse] * 2 + [lev_coarse] * 2
     scratch += [
-        dma((17,)), dma((8, NZ)), dma((8, NZ)), dma((6, ND)), dma((6, ND)), dma((8, NT)), dma((8, NT)),
+        dma((17,)), dma((8, NZ)), dma((8, NZ)), dma((6, ND)), dma((6, ND)), dma((11, NT)), dma((11, NT)),
     ]
     operands = [
         fs, leg, fold_pairs, gauss_weights, mode_rates, grid_coef, modes_to, modes_from,

time: 88.5 us -> 88.7 us (level)
  no operation moved by 1% of the time
where the time goes in v6:
time: 88.7 us; the launch traced here: 88.5 us
  Pallas kernels  86.6 us (98%)
  local copies, waits for them, and re-layouts  1.29 us (1%)
    pallas_call x1, Pallas kernels, per_device(): pl.pallas_call(kernel, out_shape=(jax.ShapeDtypeStruct((2, 2, 3, 2, ROWS)...  86.6 us

profile of v6, /device:TPU:1, one launch (start us, length us, event | category | flops | bytes accessed | tf_op | source)
XLA Modules:
  0.0 88.5 jit_solution(5881250103875097280)
XLA Ops:
  0.6 86.6 %sweep.1 = (f32[2,2,3,2,769]{4,3,2,1,0:T(2,128)S(1)}, f32[2,3,3,2,769]{4,3,2,1,0:T(2,128)S(1)}) custom-call(f32[2,3,3,2,769]{4,3,2,1,0:T(2,128)} %bitcast.7, bf16[3,769,384]{2,1,0:T(8,128)(2,1)} %bitcast.6, s32[384]{0:T(512)} %fold_hbm.1, f32[384]{0:T(512)} %gauss_hbm.1, f32[8]{0:T(128)} %rates_hbm.1, f32[8,2560]{1,0:T(8,128)} %coef_hbm.1, f32[8,8]{1,0:T(8,128)} %mto_hbm.1, ...), custom_call_target="tpu_custom_call" | custom-call | tf_op jit(solution)/shard_map/sweep/pallas_call | solution.py:563
  87.2 0.6 copy.20
  87.9 0.7 copy.21
